TPU v7x, 256 devices: a whole 4x4x8 slice. The times are simulated.
256 devices in a mesh: dp: 128 (over x, z, y), mp: 2 (over core).
Axes of the slice: x: 4, y: 4, z: 8, core: 2. Of those that a mesh axis runs over, the one named last changes fastest.
Arguments:
- view_a: bfloat16 [16384, 4096], P(('dp', 'mp')), may hold values from -500 to 500
- view_b: bfloat16 [16384, 4096], P(('dp', 'mp')), may hold values from -500 to 500
Outputs:
- grad_a: bfloat16 [16384, 4096], P(('dp', 'mp'))
- grad_b: bfloat16 [16384, 4096], P(('dp', 'mp'))
All inputs are finite; a program needn't handle non-finite values.
Results may differ from a plain program's by a relative error of at most 0.014.
Values may be sent and summed in bfloat16 or wider, within the bound.
A program may use at most 128 MiB of HBM per device.

v0:
```python
import jax
import jax.numpy as jnp
from jax import lax
from jax.sharding import PartitionSpec as P

GROUPS_A = 8


off_weight = 0.0051
epsilon = 1e-05
loss_scale = 16.0


def local(view_a, view_b):
    pair_rows = view_a.shape[0]
    features = view_a.shape[1]
    data_count = lax.axis_size("dp")
    total_rows = pair_rows * data_count * lax.axis_size("mp")
    column_groups = data_count // GROUPS_A
    width_a = features // GROUPS_A
    width_b = features // column_groups
    data_index = lax.axis_index("dp")
    tile_row = data_index // column_groups
    tile_col = data_index % column_groups
    start_a = tile_row * width_a
    start_b = tile_col * width_b
    values_a = view_a.astype(jnp.float32)
    values_b = view_b.astype(jnp.float32)
    sums_a, sums_b = lax.psum((jnp.sum(values_a, axis=0), jnp.sum(values_b, axis=0)), ("dp", "mp"))
    shifted_a = values_a - sums_a / total_rows
    shifted_b = values_b - sums_b / total_rows
    square_a, square_b = lax.psum(
        (jnp.sum(shifted_a * shifted_a, axis=0), jnp.sum(shifted_b * shifted_b, axis=0)),
        ("dp", "mp"),
    )
    rstd_a = lax.rsqrt(square_a / total_rows + epsilon)
    rstd_b = lax.rsqrt(square_b / total_rows + epsilon)
    norm_a = (shifted_a * rstd_a).astype(jnp.bfloat16)
    norm_b = (shifted_b * rstd_b).astype(jnp.bfloat16)
    send_a, send_b = (norm_a, norm_b)
    outgoing_a = jnp.repeat(
        jnp.transpose(send_a.reshape(pair_rows, GROUPS_A, width_a), (1, 0, 2)),
        column_groups,
        axis=0,
    )
    outgoing_b = jnp.tile(
        jnp.transpose(send_b.reshape(pair_rows, column_groups, width_b), (1, 0, 2)),
        (GROUPS_A, 1, 1),
    )
    arrived_a, arrived_b = (
        lax.all_to_all(outgoing_a, "dp", split_axis=0, concat_axis=0, tiled=True),
        lax.all_to_all(outgoing_b, "dp", split_axis=0, concat_axis=0, tiled=True),
    )
    half_rows = data_count * pair_rows
    tile_a = arrived_a.reshape(half_rows, width_a)
    tile_b = arrived_b.reshape(half_rows, width_b)
    tile_norm_a, tile_norm_b = (tile_a, tile_b)
    partial_corr = jnp.einsum(
        "nr,nc->rc", tile_norm_a, tile_norm_b, preferred_element_type=jnp.float32
    )
    correlation = lax.psum(partial_corr, "mp") / total_rows
    row_ids = start_a + lax.broadcasted_iota(jnp.int32, (width_a, width_b), 0)
    col_ids = start_b + lax.broadcasted_iota(jnp.int32, (width_a, width_b), 1)
    grad_corr = jnp.where(
        row_ids == col_ids, -2.0 * (1.0 - correlation), 2.0 * off_weight * correlation
    ).astype(jnp.bfloat16)
    back_a = (
        loss_scale
        * jnp.einsum("nc,rc->nr", tile_norm_b, grad_corr, preferred_element_type=jnp.float32)
    ).astype(jnp.bfloat16)
    back_b = (
        loss_scale
        * jnp.einsum("nr,rc->nc", tile_norm_a, grad_corr, preferred_element_type=jnp.float32)
    ).astype(jnp.bfloat16)
    returned_a, returned_b = (
        lax.all_to_all(
            back_a.reshape(data_count, pair_rows, width_a),
            "dp",
            split_axis=0,
            concat_axis=0,
            tiled=True,
        ),
        lax.all_to_all(
            back_b.reshape(data_count, pair_rows, width_b),
            "dp",
            split_axis=0,
            concat_axis=0,
            tiled=True,
        ),
    )
    grad_za = jnp.sum(
        returned_a.astype(jnp.float32).reshape(GROUPS_A, column_groups, pair_rows, width_a), axis=1
    )
    grad_za = jnp.transpose(grad_za, (1, 0, 2)).reshape(pair_rows, features)
    grad_zb = jnp.sum(
        returned_b.astype(jnp.float32).reshape(GROUPS_A, column_groups, pair_rows, width_b), axis=0
    )
    grad_zb = jnp.transpose(grad_zb, (1, 0, 2)).reshape(pair_rows, features)
    float_norm_a = norm_a.astype(jnp.float32)
    float_norm_b = norm_b.astype(jnp.float32)
    moment_a, moment_b = lax.psum(
        (jnp.sum(grad_za * float_norm_a, axis=0), jnp.sum(grad_zb * float_norm_b, axis=0)),
        ("dp", "mp"),
    )
    grad_a = (rstd_a * (grad_za - float_norm_a * (moment_a / total_rows))).astype(jnp.bfloat16)
    grad_b = (rstd_b * (grad_zb - float_norm_b * (moment_b / total_rows))).astype(jnp.bfloat16)
    return (grad_a, grad_b)


def solution(mesh):
    in_specs = (P(("dp", "mp"), None), P(("dp", "mp"), None))
    out_specs = (P(("dp", "mp"), None), P(("dp", "mp"), None))
    return jax.shard_map(local, mesh=mesh, in_specs=in_specs, out_specs=out_specs, check_vma=False)
```

profile of v0, /device:TPU:1, one launch (start us, length us, event | category | flops | bytes accessed | tf_op | source)
XLA Modules:
  0.0 904.2 jit_solution(7509613282068274538)
XLA Ops:
  7.2 1.1 convert_reduce_fusion.2
  8.3 1.1 convert_reduce_fusion.3
  9.5 81.6 %all-reduce.2 = (f32[4096]{0:T(1024)S(1)}, f32[4096]{0:T(1024)S(1)}) all-reduce(f32[4096]{0:T(1024)S(1)} %convert_reduce_fusion.2, f32[4096]{0:T(1024)S(1)} %convert_reduce_fusion.3), channel_id=1, replica_groups=mesh['dp'=128,'mp'=2] {'dp','mp'}, use_global_device_ids=true, to_apply=%region_5.6 | all-reduce | flops 8192 | bytes 65536 | tf_op jit(solution)/shard_map/psum | solution.py:29
  91.1 1.2 fusion.5
  92.3 1.3 fusion.7
  93.6 72.9 %all-reduce.1 = (f32[4096]{0:T(1024)S(1)}, f32[4096]{0:T(1024)S(1)}) all-reduce(f32[4096]{0:T(1024)S(1)} %fusion.5, f32[4096]{0:T(1024)S(1)} %fusion.7), channel_id=1, replica_groups=mesh['dp'=128,'mp'=2] {'dp','mp'}, use_global_device_ids=true, to_apply=%region_7.8 | all-reduce | flops 8192 | bytes 65536 | tf_op jit(solution)/shard_map/psum | solution.py:32
  166.5 1.2 fusion.6
  167.7 0.1 copy.20
  167.8 0.2 copy.13
  168.0 2.5 tile.4
  170.4 8.6 all-to-all-start
  179.0 0.1 fusion.8
  179.2 92.5 %all-to-all-done = bf16[128,64,256]{2,1,0:T(8,128)(2,1)} async-done(((bf16[128,64,256]{2,1,0:T(8,128)(2,1)}), bf16[128,64,256]{2,1,0:T(8,128)(2,1)}, u32[]{:S(2)}, u32[]{:S(2)}) %all-to-all-start) | async-done | bytes 4194336 | tf_op jit(solution)/shard_map/all_to_all | solution.py:52
  271.7 1.0 broadcast_in_dim.2
  272.7 193.3 %all_to_all.20 = bf16[128,64,512]{2,1,0:T(8,128)(2,1)S(1)} all-to-all(bf16[128,64,512]{2,1,0:T(8,128)(2,1)S(1)} %bitcast.35), channel_id=1, replica_groups=mesh['dp'=128,'mp'=2] {'dp'}, dimensions={0} | all-to-all | bytes 16777216 | tf_op jit(solution)/shard_map/all_to_all | solution.py:51
  466.1 3.2 copy-done
  469.3 5.3 convolution_bitcast_fusion
  474.7 29.4 %all-reduce.5.cloned.1.call-done = f32[512,256]{1,0:T(8,128)} async-done(((f32[512,256]{1,0:T(8,128)}), f32[512,256]{1,0:T(8,128)}) %all-reduce.5.cloned.1.call-update) | async-done | bytes 524304 | tf_op jit(solution)/shard_map/psum | solution.py:61
  504.1 7.9 fusion
  512.0 14.1 %all-to-all-start.3 = ((bf16[128,64,256]{2,1,0:T(8,128)(2,1)}), bf16[128,64,256]{2,1,0:T(8,128)(2,1)}, u32[]{:S(2)}, u32[]{:S(2)}) async-start(bf16[128,64,256]{2,1,0:T(8,128)(2,1)} %bitcast.44), calls=%async_computation.3 | async-start | bytes 8388608 | tf_op jit(solution)/shard_map/all_to_all | solution.py:83
  526.1 7.9 multiply_convert_fusion
  534.0 85.2 %all-to-all-done.3 = bf16[128,64,256]{2,1,0:T(8,128)(2,1)} async-done(((bf16[128,64,256]{2,1,0:T(8,128)(2,1)}), bf16[128,64,256]{2,1,0:T(8,128)(2,1)}, u32[]{:S(2)}, u32[]{:S(2)}) %all-to-all-start.3) | async-done | bytes 4194336 | tf_op jit(solution)/shard_map/all_to_all | solution.py:83
  619.2 11.6 %all-to-all-start.2 = ((bf16[128,64,512]{2,1,0:T(8,128)(2,1)}), bf16[128,64,512]{2,1,0:T(8,128)(2,1)}, u32[]{:S(2)}, u32[]{:S(2)}) async-start(bf16[128,64,512]{2,1,0:T(8,128)(2,1)} %bitcast.41), calls=%async_computation.2 | async-start | bytes 16777216 | tf_op jit(solution)/shard_map/all_to_all | solution.py:76
  630.9 3.0 convert_reduce_fusion.1
  633.9 0.1 copy.19
  634.0 0.2 fusion.13
  634.2 178.4 %all-to-all-done.2 = bf16[128,64,512]{2,1,0:T(8,128)(2,1)} async-done(((bf16[128,64,512]{2,1,0:T(8,128)(2,1)}), bf16[128,64,512]{2,1,0:T(8,128)(2,1)}, u32[]{:S(2)}, u32[]{:S(2)}) %all-to-all-start.2) | async-done | bytes 8388640 | tf_op jit(solution)/shard_map/all_to_all | solution.py:76
  812.6 4.8 convert_reduce_fusion
  817.5 0.2 fusion.9
  817.7 77.6 %all-reduce = (f32[4096]{0:T(1024)S(1)}, f32[4096]{0:T(1024)S(1)}) all-reduce(f32[4096]{0:T(1024)S(1)} %fusion.9, f32[4096]{0:T(1024)S(1)} %fusion.13), channel_id=1, replica_groups=mesh['dp'=128,'mp'=2] {'dp','mp'}, use_global_device_ids=true, to_apply=%region_11.12 | all-reduce | flops 8192 | bytes 65536 | tf_op jit(solution)/shard_map/psum | solution.py:101
  895.3 1.0 fusion.16
  896.3 1.0 fusion.12
  (18 shorter events, 0.2 us)
Async XLA Ops:
  92.3 86.8 %copy-start.2 = (bf16[64,4096]{1,0:T(8,128)(2,1)S(1)}, bf16[64,4096]{1,0:T(8,128)(2,1)}, u32[]{:S(2)}) copy-start(bf16[64,4096]{1,0:T(8,128)(2,1)} %param.2) | copy-start | bytes 1572868
  170.4 101.3 %all-to-all-start = ((bf16[128,64,256]{2,1,0:T(8,128)(2,1)}), bf16[128,64,256]{2,1,0:T(8,128)(2,1)}, u32[]{:S(2)}, u32[]{:S(2)}) async-start(bf16[128,64,256]{2,1,0:T(8,128)(2,1)} %bitcast.36), calls=%async_computation | async-start | bytes 8388608 | tf_op jit(solution)/shard_map/all_to_all | solution.py:52
  179.0 325.1 %all-reduce.5.cloned.1.call-start = ((), (), s32[]{:S(2)}) async-start(), calls=%async_computation.4 | async-start | bytes 1048576 | tf_op jit(solution)/shard_map/psum | solution.py:61
  466.1 3.2 copy-start
  504.1 22.0 %copy-start.3 = (f32[512,256]{1,0:T(8,128)S(1)}, f32[512,256]{1,0:T(8,128)}, u32[]{:S(2)}) copy-start(f32[512,256]{1,0:T(8,128)} %all-reduce.5.cloned.1.call-done) | copy-start | bytes 1572868
  512.0 107.2 %all-to-all-start.3 = ((bf16[128,64,256]{2,1,0:T(8,128)(2,1)}), bf16[128,64,256]{2,1,0:T(8,128)(2,1)}, u32[]{:S(2)}, u32[]{:S(2)}) async-start(bf16[128,64,256]{2,1,0:T(8,128)(2,1)} %bitcast.44), calls=%async_computation.3 | async-start | bytes 8388608 | tf_op jit(solution)/shard_map/all_to_all | solution.py:83
  619.2 14.8 %copy-start.1 = (bf16[64,4096]{1,0:T(8,128)(2,1)S(1)}, bf16[64,4096]{1,0:T(8,128)(2,1)}, u32[]{:S(2)}) copy-start(bf16[64,4096]{1,0:T(8,128)(2,1)} %param.3) | copy-start | bytes 1572868
  619.2 193.4 %all-to-all-start.2 = ((bf16[128,64,512]{2,1,0:T(8,128)(2,1)}), bf16[128,64,512]{2,1,0:T(8,128)(2,1)}, u32[]{:S(2)}, u32[]{:S(2)}) async-start(bf16[128,64,512]{2,1,0:T(8,128)(2,1)} %bitcast.41), calls=%async_computation.2 | async-start | bytes 16777216 | tf_op jit(solution)/shard_map/all_to_all | solution.py:76
Sparse Core Ops, SparseCore 0:
  474.8 29.2 all-reduce.4
where the time goes:
time: 905 us; the launch traced here: 904 us
  blocking collectives  425 us (47%)
  waiting for transfers between devices  385 us (43%)
  starting transfers between devices  34.3 us (4%)
  matrix products  21.1 us (2%)
  other arithmetic  16.4 us (2%)
  between operations  14.2 us (2%)
    all_to_all x1, blocking collectives, local(): lax.all_to_all(outgoing_a, 'dp', split_axis=0, concat_axis=0, tiled=True)  193 us
    all_to_all x1, waiting for transfers between devices, local(): lax.all_to_all(back_a.reshape(data_count, pair_rows, width_a), 'dp', spli...  178 us
    all_to_all x1, waiting for transfers between devices, local(): lax.all_to_all(outgoing_b, 'dp', split_axis=0, concat_axis=0, tiled=True)  92.5 us
    all_to_all x1, waiting for transfers between devices, local(): lax.all_to_all(back_b.reshape(data_count, pair_rows, width_b), 'dp', spli...  85.2 us
    psum x1, blocking collectives, local(): lax.psum((jnp.sum(values_a, axis=0), jnp.sum(values_b, axis=0)), ('dp', '...  81.6 us
    psum x1, blocking collectives, local(): lax.psum((jnp.sum(grad_za * float_norm_a, axis=0), jnp.sum(grad_zb * floa...  77.6 us
    psum x1, blocking collectives, local(): lax.psum((jnp.sum(shifted_a * shifted_a, axis=0), jnp.sum(shifted_b * shi...  72.9 us
    psum x1, waiting for transfers between devices, local(): correlation = lax.psum(partial_corr, 'mp') / total_rows  29.4 us
  transfers between devices with their start and end apart: 4, of which 4 were waited for; matrix products, arithmetic and copies ran while one was open for 1% of the time, Pallas kernels for 0%

commit v1 on v0

v1 whole, which is shorter than its diff:
```python
import jax
import jax.numpy as jnp
from jax import lax
from jax.experimental import pallas as pl
from jax.experimental.pallas import tpu as pltpu
from jax.sharding import PartitionSpec as P

NX, NY, NZ, NC = 4, 4, 8, 2
R = 64
D = 4096
W = 1024
H = 512
Q = 128
N = 16384
OFF_WEIGHT = 0.0051
EPS = 1e-05
SCALE = 16.0
F32 = jnp.float32
BF16 = jnp.bfloat16
MESH = pl.DeviceIdType.MESH

_SIZES = dict(
    A=16, B=16, S1A=4, S1B=4, S2A=4, S2B=4, S3=16, CX=4,
    ZP=8, ZM=8, G=16, GX=16, MO=16, MA=4, MB=4,
    AP=6, AM=6, BP=6, BM=6, OA=4, OB=4, LOC=2,
)
SEM = {}
_n = 0
for _k, _v in _SIZES.items():
    SEM[_k] = _n
    _n += _v
N_RECV = _n
N_SEND = 260


def kernel(a_in, b_in, ga, gb, RA, RB, TA, TB, S0A, S0B, S1A, S1B, S2A, S2B, S3, FIN,
           CS, CO, CR, P0, P, M0, M, GT, MO, MA, MB, PA, PB, AP0, AP, AM0, AM, BP0, BP, BM0, BM,
           SA, SB, ssem, rsem):
    me = lax.axis_index("dp")
    c = lax.axis_index("mp")
    x = me // (NZ * NY)
    z = (me // NY) % NZ
    y = me % NY
    o = 1 - c

    def dev(xx, yy, zz, cc):
        return {"dp": xx * (NZ * NY) + zz * NY + yy, "mp": cc}

    def wrap(v, n):
        return (v + n) % n

    peers = [dev(wrap(x + k, NX), y, z, c) for k in range(1, NX)]
    peers += [dev(x, wrap(y + k, NY), z, c) for k in range(1, NY)]
    zc = [(k, s) for k in range(NZ) for s in range(NC) if (k, s) != (0, 0)]
    zc_peers = [dev(x, y, wrap(z + k, NZ), (c + s) % NC) for k, s in zc]
    peers += zc_peers
    barrier = pltpu.get_barrier_semaphore()
    for p in peers:
        pl.semaphore_signal(barrier, inc=1, device_id=p, device_id_type=MESH)
    pl.semaphore_wait(barrier, len(peers))

    xp, xm = dev(wrap(x + 1, NX), y, z, c), dev(wrap(x - 1, NX), y, z, c)
    yp, ym = dev(x, wrap(y + 1, NY), z, c), dev(x, wrap(y - 1, NY), z, c)
    zp, zm = dev(x, y, wrap(z + 1, NZ), c), dev(x, y, wrap(z - 1, NZ), c)
    sib = dev(x, y, z, o)

    sent = []

    def send(src, dst, fam, idx, to):
        cp = pltpu.make_async_remote_copy(
            src_ref=src, dst_ref=dst, send_sem=ssem.at[len(sent)], recv_sem=rsem.at[SEM[fam] + idx],
            device_id=to, device_id_type=MESH)
        cp.start()
        sent.append(cp)

    def recv(dst, fam, idx):
        pltpu.make_async_remote_copy(
            src_ref=dst, dst_ref=dst, send_sem=ssem.at[0], recv_sem=rsem.at[SEM[fam] + idx],
            device_id=sib, device_id_type=MESH).wait_recv()

    def cols(i, w=W):
        return pl.ds(pl.multiple_of(i * w, w), w)

    def slot(xx, yy):
        return xx * NY + yy

    def rows(s):
        return pl.ds(pl.multiple_of(s * R, R), R)

    own = slot(x, y)
    for k in (2, 1, 3):
        t = wrap(x + k, NX)
        send(a_in.at[:, cols(t)], RA.at[own], "A", own, dev(t, y, z, c))
        t = wrap(y + k, NY)
        send(b_in.at[:, cols(t)], RB.at[own], "B", own, dev(x, t, z, c))
    send(a_in.at[:, cols(x)], RA.at[own], "A", own, yp)
    send(a_in.at[:, cols(x)], RA.at[own], "A", own, ym)
    send(b_in.at[:, cols(y)], RB.at[own], "B", own, xp)
    send(b_in.at[:, cols(y)], RB.at[own], "B", own, xm)
    la = pltpu.make_async_copy(a_in.at[:, cols(x)], RA.at[own], rsem.at[SEM["LOC"]])
    lb = pltpu.make_async_copy(b_in.at[:, cols(y)], RB.at[own], rsem.at[SEM["LOC"] + 1])
    la.start()
    lb.start()

    def local_stats(v_ref, s_ref):
        for i in range(4):
            v = v_ref[:, i * W:(i + 1) * W].astype(F32)
            m = jnp.sum(v, axis=0, keepdims=True) * (1.0 / R)
            d = v - m
            s_ref[i, 0:1, :] = m
            s_ref[i, 1:2, :] = jnp.sum(d * d, axis=0, keepdims=True)

    local_stats(a_in, S0A)
    local_stats(b_in, S0B)
    for k in (2, 1, 3):
        t = wrap(x + k, NX)
        send(S0A.at[t], S1A.at[x], "S1A", x, dev(t, y, z, c))
        t = wrap(y + k, NY)
        send(S0B.at[t], S1B.at[y], "S1B", y, dev(x, t, z, c))
    S1A[x] = S0A[x]
    S1B[y] = S0B[y]

    def merge(parts, n):
        mean = parts[0][0]
        for m, _ in parts[1:]:
            mean = mean + m
        mean = mean * (1.0 / len(parts))
        total = None
        for m, q in parts:
            d = m - mean
            t = q + n * (d * d)
            total = t if total is None else total + t
        return mean, total

    la.wait()
    lb.wait()
    for k in (1, 3, 2):
        s = slot(wrap(x + k, NX), y)
        recv(RA.at[s], "A", s)
        send(RA.at[s], RA.at[s], "A", s, yp)
        send(RA.at[s], RA.at[s], "A", s, ym)
        s = slot(x, wrap(y + k, NY))
        recv(RB.at[s], "B", s)
        send(RB.at[s], RB.at[s], "B", s, xp)
        send(RB.at[s], RB.at[s], "B", s, xm)

    for k in (1, 3, 2):
        recv(S1A.at[wrap(x + k, NX)], "S1A", wrap(x + k, NX))
        recv(S1B.at[wrap(y + k, NY)], "S1B", wrap(y + k, NY))
    mean, m2 = merge([(S1A[k, 0:1, :], S1A[k, 1:2, :]) for k in range(4)], float(R))
    S2A[y, 0:1, :] = mean
    S2A[y, 1:2, :] = m2
    mean, m2 = merge([(S1B[k, 0:1, :], S1B[k, 1:2, :]) for k in range(4)], float(R))
    S2B[x, 0:1, :] = mean
    S2B[x, 1:2, :] = m2
    for k in (2, 1, 3):
        send(S2A.at[y], S2A.at[y], "S2A", y, dev(x, wrap(y + k, NY), z, c))
        send(S2B.at[x], S2B.at[x], "S2B", x, dev(wrap(x + k, NX), y, z, c))

    for k in (0, 1):
        s = slot(wrap(x + k, NX), wrap(y - 1, NY))
        recv(RA.at[s], "A", s)
        if k == 0:
            send(RA.at[s], RA.at[s], "A", s, yp)
        s = slot(wrap(x + k, NX), wrap(y + 1, NY))
        recv(RA.at[s], "A", s)
        if k == 1:
            send(RA.at[s], RA.at[s], "A", s, ym)
        s = slot(wrap(x - 1, NX), wrap(y + k, NY))
        recv(RB.at[s], "B", s)
        if k == 0:
            send(RB.at[s], RB.at[s], "B", s, xp)
        s = slot(wrap(x + 1, NX), wrap(y + k, NY))
        recv(RB.at[s], "B", s)
        if k == 1:
            send(RB.at[s], RB.at[s], "B", s, xm)

    for k in (1, 3, 2):
        recv(S2A.at[wrap(y + k, NY)], "S2A", wrap(y + k, NY))
        recv(S2B.at[wrap(x + k, NX)], "S2B", wrap(x + k, NX))
    mine = z * NC + c
    mean, m2 = merge([(S2A[k, 0:1, :], S2A[k, 1:2, :]) for k in range(4)], 4.0 * R)
    S3[mine, 0:1, :] = mean
    S3[mine, 1:2, :] = m2
    mean, m2 = merge([(S2B[k, 0:1, :], S2B[k, 1:2, :]) for k in range(4)], 4.0 * R)
    S3[mine, 2:3, :] = mean
    S3[mine, 3:4, :] = m2
    for p in zc_peers:
        send(S3.at[mine], S3.at[mine], "S3", mine, p)

    for k in (3, 2):
        s = slot(wrap(x + k, NX), wrap(y - 1, NY))
        recv(RA.at[s], "A", s)
        if k == 2:
            send(RA.at[s], RA.at[s], "A", s, yp)
        s = slot(wrap(x + k, NX), wrap(y + 1, NY))
        recv(RA.at[s], "A", s)
        if k == 3:
            send(RA.at[s], RA.at[s], "A", s, ym)
        s = slot(wrap(x - 1, NX), wrap(y + k, NY))
        recv(RB.at[s], "B", s)
        if k == 2:
            send(RB.at[s], RB.at[s], "B", s, xp)
        s = slot(wrap(x + 1, NX), wrap(y + k, NY))
        recv(RB.at[s], "B", s)
        if k == 3:
            send(RB.at[s], RB.at[s], "B", s, xm)

    for k, s in zc:
        i = wrap(z + k, NZ) * NC + (c + s) % NC
        recv(S3.at[i], "S3", i)
    for v in range(2):
        mean, m2 = merge([(S3[k, 2 * v:2 * v + 1, :], S3[k, 2 * v + 1:2 * v + 2, :]) for k in range(16)], 16.0 * R)
        FIN[2 * v:2 * v + 1, :] = mean
        FIN[2 * v + 1:2 * v + 2, :] = lax.rsqrt(m2 * (1.0 / N) + EPS)

    def norm_a(s):
        v = (RA[s].astype(F32) - FIN[0:1, :]) * FIN[1:2, :]
        TA[rows(s), :] = v.astype(BF16)

    def norm_b(s):
        v = (RB[s].astype(F32) - FIN[2:3, :]) * FIN[3:4, :]
        TB[rows(s), :] = v.astype(BF16)

    def early(i, _):
        k = i // 3
        h = (i % 3 + 3) % 4
        norm_a(slot(k, wrap(y + h, NY)))
        norm_b(slot(wrap(x + h, NX), k))
        return 0

    lax.fori_loop(0, 12, early, 0)
    for k in (0, 1, 3, 2):
        s = slot(wrap(x + k, NX), wrap(y + 2, NY))
        recv(RA.at[s], "A", s)
        norm_a(s)
        s = slot(wrap(x + 2, NX), wrap(y + k, NY))
        recv(RB.at[s], "B", s)
        norm_b(s)

    def corr(t, half):
        lhs = TA[:, cols(t, 2 * Q)]
        rhs = TB[:, cols(half, H)]
        return lax.dot_general(lhs, rhs, (((0,), (0,)), ((), ())), preferred_element_type=F32)

    def pair(t):
        return pl.ds(pl.multiple_of(t * 2, 2), 2)

    zt = z // 2
    for k in (2, 1, 3, 0):
        t = (zt + k) % 4
        CS[pair(t)] = corr(t, o).reshape(2, Q, H)
        send(CS.at[pair(t)], CR.at[pair(t)], "CX", t, sib)

    def own_half(k, _):
        t = (zt + k) % 4
        CO[pair(t)] = corr(t, c).reshape(2, Q, H)
        return 0

    lax.fori_loop(0, 4, own_half, 0)
    for k in (2, 1, 3, 0):
        t = (zt + k) % 4
        recv(CR.at[pair(t)], "CX", t)

    def add_other(k, _):
        CO[k] = CO[k] + CR[k]
        return 0

    lax.fori_loop(0, 8, add_other, 0)

    lo, hi = pl.ds(0, R), pl.ds(R, R)
    q4 = (z + 4) % NZ
    send(CO.at[q4, lo], P0, "ZP", 0, zp)
    send(CO.at[q4, hi], M0, "ZM", 0, zm)
    q3p, q3m = wrap(z + 3, NZ), wrap(z - 3, NZ)
    send(CO.at[q3p, hi], P.at[0, hi], "ZP", 1, zp)
    send(CO.at[q3m, lo], M.at[0, lo], "ZM", 1, zm)
    recv(P0, "ZP", 0)
    CO[q3p, lo] = CO[q3p, lo] + P0[...]
    send(CO.at[q3p, lo], P.at[0, lo], "ZP", 2, zp)
    recv(M0, "ZM", 0)
    CO[q3m, hi] = CO[q3m, hi] + M0[...]
    send(CO.at[q3m, hi], M.at[0, hi], "ZM", 2, zm)
    for j in (1, 2):
        qp, qm = wrap(z + 3 - j, NZ), wrap(z - 3 + j, NZ)
        for part, (sp, sm) in enumerate(((hi, lo), (lo, hi))):
            recv(P.at[j - 1, sp], "ZP", 2 * j - 1 + part)
            CO[qp, sp] = CO[qp, sp] + P[j - 1, sp]
            send(CO.at[qp, sp], P.at[j, sp], "ZP", 2 * j + 1 + part, zp)
            recv(M.at[j - 1, sm], "ZM", 2 * j - 1 + part)
            CO[qm, sm] = CO[qm, sm] + M[j - 1, sm]
            send(CO.at[qm, sm], M.at[j, sm], "ZM", 2 * j + 1 + part, zm)
    for part, (sp, sm) in enumerate(((hi, lo), (lo, hi))):
        recv(P.at[2, sp], "ZP", 5 + part)
        recv(M.at[2, sm], "ZM", 5 + part)
    cc = (CO[z] + (P[2] + M[2])) * (1.0 / N)

    ri = x * W + z * Q + lax.broadcasted_iota(jnp.int32, (Q, H), 0)
    ci = y * W + c * H + lax.broadcasted_iota(jnp.int32, (Q, H), 1)
    g = jnp.where(ri == ci, -2.0 * (1.0 - cc), (2.0 * OFF_WEIGHT) * cc).astype(BF16)
    GT[c, rowsq(z)] = g
    for part in (lo, hi):
        src = GT.at[c, pl.ds(pl.multiple_of(z * Q + part.start, R), R)]
        send(src, src, "G", 2 * z + part.start // R, zp)
        send(src, src, "G", 2 * z + part.start // R, zm)
    src = GT.at[c, rowsq(z)]
    send(src, src, "GX", c * NZ + z, sib)

    prod = g.astype(F32) * cc
    csum = jnp.sum(prod, axis=0, keepdims=True)
    for k in range(4):
        MO[mine, k:k + 1, :] = csum[:, k * 128:(k + 1) * 128]
    fold = prod[:, 0:128] + prod[:, 128:256] + prod[:, 256:384] + prod[:, 384:512]
    MO[mine, 4:5, :] = jnp.sum(fold.T, axis=0, keepdims=True)
    MO[mine, 5:8, :] = jnp.zeros((3, 128), F32)
    for p in zc_peers:
        send(MO.at[mine], MO.at[mine], "MO", mine, p)

    def gpart(q, h):
        return GT.at[c, pl.ds(pl.multiple_of(q * Q + h * R, R), R)]

    for j in (1, 2, 3):
        for sgn, to in ((-1, zp), (1, zm)):
            q = wrap(z + sgn * j, NZ)
            for h in (0, 1):
                recv(gpart(q, h), "G", 2 * q + h)
                if j < 3 or (h == 0 if sgn < 0 else h == 1):
                    send(gpart(q, h), gpart(q, h), "G", 2 * q + h, to)
            src = GT.at[c, rowsq(q)]
            send(src, src, "GX", c * NZ + q, sib)
    for h in (0, 1):
        recv(gpart(q4, h), "G", 2 * q4 + h)
    src = GT.at[c, rowsq(q4)]
    send(src, src, "GX", c * NZ + q4, sib)

    for k, s in zc:
        i = wrap(z + k, NZ) * NC + (c + s) % NC
        recv(MO.at[i], "MO", i)
    for q in range(NZ):
        MA[y, 0:1, q * Q:(q + 1) * Q] = MO[2 * q, 4:5, :] + MO[2 * q + 1, 4:5, :]
    for h in range(2):
        for k in range(4):
            t = MO[h, k:k + 1, :]
            for q in range(1, NZ):
                t = t + MO[2 * q + h, k:k + 1, :]
            MB[x, 0:1, h * H + k * 128:h * H + (k + 1) * 128] = t
    for k in (2, 1, 3):
        send(MA.at[y], MA.at[y], "MA", y, dev(x, wrap(y + k, NY), z, c))
        send(MB.at[x], MB.at[x], "MB", x, dev(wrap(x + k, NX), y, z, c))

    for q in range(NZ):
        qq = wrap(z - q, NZ)
        dst = GT.at[o, rowsq(qq)]
        recv(dst, "GX", o * NZ + qq)

    def term_a(yy):
        lhs = jnp.concatenate([TB[rows(slot(k, yy)), :] for k in range(4)], axis=0)
        t = lax.dot_general(lhs[:, :H], GT[0], (((1,), (1,)), ((), ())), preferred_element_type=F32)
        t = t + lax.dot_general(lhs[:, H:], GT[1], (((1,), (1,)), ((), ())), preferred_element_type=F32)
        return SCALE * t

    def term_b(xx):
        lhs = TA[pl.ds(pl.multiple_of(xx * 4 * R, 4 * R), 4 * R), :]
        return SCALE * jnp.concatenate(
            [jnp.dot(lhs, GT[h], preferred_element_type=F32) for h in range(2)], axis=1)

    sides = (
        (term_a, y, NY, PA, AP0, AP, AM0, AM, "AP", "AM", yp, ym),
        (term_b, x, NX, PB, BP0, BP, BM0, BM, "BP", "BM", xp, xm),
    )
    for term, pos, n, buf, p0, p1, m0, m1, fp, fm, to_p, to_m in sides:
        buf[2] = term(wrap(pos + 2, n)).astype(BF16).reshape(4, R, W)
        for k in range(2):
            send(buf.at[2, k], p0.at[k], fp, k, to_p)
            send(buf.at[2, 2 + k], m0.at[k], fm, k, to_m)
    for term, pos, n, buf, p0, p1, m0, m1, fp, fm, to_p, to_m in sides:
        buf[0] = term(wrap(pos + 1, n)).astype(BF16).reshape(4, R, W)
        for k in (2, 3):
            send(buf.at[0, k], p1.at[k], fp, 2 + k, to_p)
        for k in range(2):
            recv(p0.at[k], fp, k)
            buf[0, k] = (buf[0, k].astype(F32) + p0[k].astype(F32)).astype(BF16)
            send(buf.at[0, k], p1.at[k], fp, 2 + k, to_p)
        buf[1] = term(wrap(pos - 1, n)).astype(BF16).reshape(4, R, W)
        for k in range(2):
            send(buf.at[1, k], m1.at[k], fm, 2 + k, to_m)
        for k in range(2):
            recv(m0.at[k], fm, k)
            buf[1, 2 + k] = (buf[1, 2 + k].astype(F32) + m0[k].astype(F32)).astype(BF16)
            send(buf.at[1, 2 + k], m1.at[2 + k], fm, 4 + k, to_m)

    for k in (1, 3, 2):
        recv(MA.at[wrap(y + k, NY)], "MA", wrap(y + k, NY))
        recv(MB.at[wrap(x + k, NX)], "MB", wrap(x + k, NX))
    mom_a = ((MA[0] + MA[1]) + (MA[2] + MA[3])) * SCALE
    mom_b = ((MB[0] + MB[1]) + (MB[2] + MB[3])) * SCALE

    buf_a = term_a(y).astype(BF16)
    buf_b = term_b(x).astype(BF16)
    PA[3] = buf_a.reshape(4, R, W)
    PB[3] = buf_b.reshape(4, R, W)
    for k in range(4):
        recv(AP.at[k], "AP", 2 + k)
        recv(AM.at[k], "AM", 2 + k)
        back = PA[3, k].astype(F32) + (AP[k].astype(F32) + AM[k].astype(F32))
        SA[k] = (FIN[1:2, :] * (back - TA[rows(slot(k, y)), :].astype(F32) * mom_a)).astype(BF16)
        recv(BP.at[k], "BP", 2 + k)
        recv(BM.at[k], "BM", 2 + k)
        back = PB[3, k].astype(F32) + (BP[k].astype(F32) + BM[k].astype(F32))
        SB[k] = (FIN[3:4, :] * (back - TB[rows(slot(x, k)), :].astype(F32) * mom_b)).astype(BF16)
    for k in (2, 1, 3):
        t = wrap(x + k, NX)
        send(SA.at[t], ga.at[:, cols(x)], "OA", x, dev(t, y, z, c))
        t = wrap(y + k, NY)
        send(SB.at[t], gb.at[:, cols(y)], "OB", y, dev(x, t, z, c))
    ga[:, cols(x)] = SA[x]
    gb[:, cols(y)] = SB[y]
    for k in (1, 3, 2):
        t = wrap(x + k, NX)
        recv(ga.at[:, cols(t)], "OA", t)
        t = wrap(y + k, NY)
        recv(gb.at[:, cols(t)], "OB", t)
    for cp in sent:
        cp.wait_send()


def rowsq(q):
    return pl.ds(pl.multiple_of(q * Q, Q), Q)


def local(view_a, view_b):
    V = pltpu.VMEM
    scratch = [
        V((16, R, W), BF16), V((16, R, W), BF16),
        V((16 * R, W), BF16), V((16 * R, W), BF16),
        V((4, 2, W), F32), V((4, 2, W), F32),
        V((4, 2, W), F32), V((4, 2, W), F32),
        V((4, 2, W), F32), V((4, 2, W), F32),
        V((16, 4, W), F32), V((4, W), F32),
        V((NZ, Q, H), F32), V((NZ, Q, H), F32), V((NZ, Q, H), F32),
        V((R, H), F32), V((3, Q, H), F32), V((R, H), F32), V((3, Q, H), F32),
        V((2, W, H), BF16),
        V((16, 8, 128), F32), V((4, 1, W), F32), V((4, 1, W), F32),
        V((4, 4, R, W), BF16), V((4, 4, R, W), BF16),
        V((2, R, W), BF16), V((4, R, W), BF16), V((2, R, W), BF16), V((4, R, W), BF16),
        V((2, R, W), BF16), V((4, R, W), BF16), V((2, R, W), BF16), V((4, R, W), BF16),
        V((4, R, W), BF16), V((4, R, W), BF16),
        pltpu.SemaphoreType.DMA((N_SEND,)),
        pltpu.SemaphoreType.DMA((N_RECV,)),
    ]
    out = jax.ShapeDtypeStruct((R, D), BF16)
    return tuple(pl.pallas_call(
        kernel,
        out_shape=(out, out),
        in_specs=[pl.BlockSpec(memory_space=pltpu.VMEM)] * 2,
        out_specs=(pl.BlockSpec(memory_space=pltpu.VMEM),) * 2,
        scratch_shapes=scratch,
        compiler_params=pltpu.CompilerParams(
            collective_id=0, has_side_effects=True, vmem_limit_bytes=56 * 1024 * 1024),
    )(view_a, view_b))


def solution(mesh):
    spec = P(("dp", "mp"), None)
    return jax.shard_map(local, mesh=mesh, in_specs=(spec, spec), out_specs=(spec, spec), check_vma=False)
```

time: 905 us -> 127 us (0.14)
  blocking collectives: 425 us -> 0 us
  waiting for transfers between devices: 385 us -> 0 us
  Pallas kernels: 0 us -> 123 us
  starting transfers between devices: 34.3 us -> 0 us
  matrix products: 21.1 us -> 0 us
  other arithmetic: 16.4 us -> 0 us
  between operations: 14.2 us -> 0.65 us
    all_to_all x3 -> x0, waiting for transfers between devices: 356 us -> none  [the longest x1 178 us: local(): lax.all_to_all(back_a.reshape(data_count, pair_rows, width_a), 'dp', spli...]
    psum x3 -> x0, blocking collectives: 232 us -> none  [the longest x1 81.6 us: local(): lax.psum((jnp.sum(values_a, axis=0), jnp.sum(values_b, axis=0)), ('dp', '...]
    all_to_all x1 -> x0, blocking collectives: 193 us -> none  [local(): lax.all_to_all(outgoing_a, 'dp', split_axis=0, concat_axis=0, tiled=True)]
    pallas_call x0 -> x1, Pallas kernels: none -> 123 us  [local(): pl.pallas_call(kernel, out_shape=(out, out), in_specs=[pl.BlockSpec(memor...]
    all_to_all x3 -> x0, starting transfers between devices: 34.3 us -> none  [the longest x1 14.1 us: local(): lax.all_to_all(back_b.reshape(data_count, pair_rows, width_b), 'dp', spli...]
    psum x1 -> x0, waiting for transfers between devices: 29.4 us -> none  [local(): correlation = lax.psum(partial_corr, 'mp') / total_rows]
    dot_general x3 -> x0, matrix products: 21.1 us -> none  [the longest x1 7.91 us: local(): jnp.einsum('nr,rc->nc', tile_norm_a, grad_corr, preferred_element_type=jn...]
    reduce_sum x8 -> x0, other arithmetic: 13 us -> none  [the longest x1 4.84 us: local(): jnp.sum(returned_a.astype(jnp.float32).reshape(GROUPS_A, column_groups, p...]
  transfers between devices with their start and end apart: 4 -> 0, of which waited for: 4 -> 0; matrix products, arithmetic and copies ran while one was open for 1% -> 0% of each run, Pallas kernels for 0% -> 0%
where the time goes in v1:
time: 127 us; the launch traced here: 126 us
  Pallas kernels  123 us (97%)
  local copies, waits for them, and re-layouts  2.72 us (2%)
    pallas_call x1, Pallas kernels, local(): pl.pallas_call(kernel, out_shape=(out, out), in_specs=[pl.BlockSpec(memor...  123 us
    unnamed x4, local copies, waits for them, and re-layouts  2.72 us

profile of v1, /device:TPU:1, one launch (start us, length us, event | category | flops | bytes accessed | tf_op | source)
XLA Modules:
  0.0 126.4 jit_solution(10932283402315211873)
XLA Ops:
  0.6 123.1 %shard_map.41 = (bf16[64,4096]{1,0:T(8,128)(2,1)}, bf16[64,4096]{1,0:T(8,128)(2,1)}) custom-call(bf16[64,4096]{1,0:T(8,128)(2,1)} %a_in.1, bf16[64,4096]{1,0:T(8,128)(2,1)} %b_in.1), custom_call_target="tpu_custom_call" | custom-call | tf_op jit(solution)/shard_map/pallas_call | solution.py:452
  123.7 0.0 copy-start
  123.7 1.9 %copy.6 = bf16[64,4096]{1,0:T(8,128)(2,1)} copy(bf16[64,4096]{1,0:T(8,128)(2,1)} %get-tuple-element.4) | data formatting | bytes 1048576
  125.7 0.0 copy-done
  125.7 0.8 copy.7
Async XLA Ops:
  123.7 1.9 %copy-start = (bf16[64,4096]{1,0:T(8,128)(2,1)S(1)}, bf16[64,4096]{1,0:T(8,128)(2,1)}, u32[]{:S(2)}) copy-start(bf16[64,4096]{1,0:T(8,128)(2,1)} %get-tuple-element.5) | copy-start | bytes 1572868

commit v2 on v1

--- a/solution.py
+++ b/solution.py
@@ -21,7 +21,7 @@
 
 _SIZES = dict(
     A=16, B=16, S1A=4, S1B=4, S2A=4, S2B=4, S3=16, CX=4,
-    ZP=8, ZM=8, G=16, GX=16, MO=16, MA=4, MB=4,
+    ZP=7, ZM=7, DV=8, G=16, GX=16, MO=16, MA=4, MB=4,
     AP=6, AM=6, BP=6, BM=6, OA=4, OB=4, LOC=2,
 )
 SEM = {}
@@ -30,11 +30,11 @@
     SEM[_k] = _n
     _n += _v
 N_RECV = _n
-N_SEND = 260
-
-
-def kernel(a_in, b_in, ga, gb, RA, RB, TA, TB, S0A, S0B, S1A, S1B, S2A, S2B, S3, FIN,
-           CS, CO, CR, P0, P, M0, M, GT, MO, MA, MB, PA, PB, AP0, AP, AM0, AM, BP0, BP, BM0, BM,
+N_SEND = 280
+
+
+def kernel(a_hbm, b_hbm, ga, gb, a_in, b_in, RA, RB, TA, TB, S0A, S0B, S1A, S1B, S2A, S2B, S3, FIN,
+           CS, CO, CR, P0, P, M0, M, ZP, ZM, DS, DV, GT, MO, MA, MB, PA, PB, AP0, AP, AM0, AM, BP0, BP, BM0, BM,
            SA, SB, ssem, rsem):
     me = lax.axis_index("dp")
     c = lax.axis_index("mp")
@@ -57,7 +57,10 @@
     barrier = pltpu.get_barrier_semaphore()
     for p in peers:
         pl.semaphore_signal(barrier, inc=1, device_id=p, device_id_type=MESH)
-    pl.semaphore_wait(barrier, len(peers))
+    la = pltpu.make_async_copy(a_hbm, a_in, rsem.at[SEM["LOC"]])
+    lb = pltpu.make_async_copy(b_hbm, b_in, rsem.at[SEM["LOC"] + 1])
+    la.start()
+    lb.start()
 
     xp, xm = dev(wrap(x + 1, NX), y, z, c), dev(wrap(x - 1, NX), y, z, c)
     yp, ym = dev(x, wrap(y + 1, NY), z, c), dev(x, wrap(y - 1, NY), z, c)
@@ -87,7 +90,23 @@
     def rows(s):
         return pl.ds(pl.multiple_of(s * R, R), R)
 
+    def local_stats(v_ref, s_ref):
+        for i in range(4):
+            v = v_ref[:, i * W:(i + 1) * W].astype(F32)
+            m = jnp.sum(v, axis=0, keepdims=True) * (1.0 / R)
+            d = v - m
+            s_ref[i, 0:1, :] = m
+            s_ref[i, 1:2, :] = jnp.sum(d * d, axis=0, keepdims=True)
+
     own = slot(x, y)
+    la.wait()
+    local_stats(a_in, S0A)
+    RA[own] = a_in[:, cols(x)]
+    lb.wait()
+    local_stats(b_in, S0B)
+    RB[own] = b_in[:, cols(y)]
+    pl.semaphore_wait(barrier, len(peers))
+
     for k in (2, 1, 3):
         t = wrap(x + k, NX)
         send(a_in.at[:, cols(t)], RA.at[own], "A", own, dev(t, y, z, c))
@@ -97,21 +116,6 @@
     send(a_in.at[:, cols(x)], RA.at[own], "A", own, ym)
     send(b_in.at[:, cols(y)], RB.at[own], "B", own, xp)
     send(b_in.at[:, cols(y)], RB.at[own], "B", own, xm)
-    la = pltpu.make_async_copy(a_in.at[:, cols(x)], RA.at[own], rsem.at[SEM["LOC"]])
-    lb = pltpu.make_async_copy(b_in.at[:, cols(y)], RB.at[own], rsem.at[SEM["LOC"] + 1])
-    la.start()
-    lb.start()
-
-    def local_stats(v_ref, s_ref):
-        for i in range(4):
-            v = v_ref[:, i * W:(i + 1) * W].astype(F32)
-            m = jnp.sum(v, axis=0, keepdims=True) * (1.0 / R)
-            d = v - m
-            s_ref[i, 0:1, :] = m
-            s_ref[i, 1:2, :] = jnp.sum(d * d, axis=0, keepdims=True)
-
-    local_stats(a_in, S0A)
-    local_stats(b_in, S0B)
     for k in (2, 1, 3):
         t = wrap(x + k, NX)
         send(S0A.at[t], S1A.at[x], "S1A", x, dev(t, y, z, c))
@@ -132,8 +136,6 @@
             total = t if total is None else total + t
         return mean, total
 
-    la.wait()
-    lb.wait()
     for k in (1, 3, 2):
         s = slot(wrap(x + k, NX), y)
         recv(RA.at[s], "A", s)
@@ -247,62 +249,97 @@
         return pl.ds(pl.multiple_of(t * 2, 2), 2)
 
     zt = z // 2
-    for k in (2, 1, 3, 0):
+    lo, hi = pl.ds(0, R), pl.ds(R, R)
+    eye = (lax.broadcasted_iota(jnp.int32, (Q, Q), 0) == lax.broadcasted_iota(jnp.int32, (Q, Q), 1)).astype(F32)
+
+    def give(k):
         t = (zt + k) % 4
         CS[pair(t)] = corr(t, o).reshape(2, Q, H)
         send(CS.at[pair(t)], CR.at[pair(t)], "CX", t, sib)
 
-    def own_half(k, _):
+    def keep(k):
         t = (zt + k) % 4
         CO[pair(t)] = corr(t, c).reshape(2, Q, H)
-        return 0
-
-    lax.fori_loop(0, 4, own_half, 0)
-    for k in (2, 1, 3, 0):
+
+    def add(k):
         t = (zt + k) % 4
         recv(CR.at[pair(t)], "CX", t)
 
-    def add_other(k, _):
-        CO[k] = CO[k] + CR[k]
-        return 0
-
-    lax.fori_loop(0, 8, add_other, 0)
-
-    lo, hi = pl.ds(0, R), pl.ds(R, R)
+        def body(i, _):
+            q = 2 * t + i
+            CO[q] = CO[q] + CR[q]
+            block = CO[q, :, pl.ds(pl.multiple_of((q % 4) * Q, Q), Q)]
+            DS[q] = jnp.sum(block * eye, axis=0, keepdims=True)
+            return 0
+
+        lax.fori_loop(0, 2, body, 0)
+
     q4 = (z + 4) % NZ
-    send(CO.at[q4, lo], P0, "ZP", 0, zp)
-    send(CO.at[q4, hi], M0, "ZM", 0, zm)
-    q3p, q3m = wrap(z + 3, NZ), wrap(z - 3, NZ)
-    send(CO.at[q3p, hi], P.at[0, hi], "ZP", 1, zp)
-    send(CO.at[q3m, lo], M.at[0, lo], "ZM", 1, zm)
-    recv(P0, "ZP", 0)
-    CO[q3p, lo] = CO[q3p, lo] + P0[...]
-    send(CO.at[q3p, lo], P.at[0, lo], "ZP", 2, zp)
-    recv(M0, "ZM", 0)
-    CO[q3m, hi] = CO[q3m, hi] + M0[...]
-    send(CO.at[q3m, hi], M.at[0, hi], "ZM", 2, zm)
-    for j in (1, 2):
+    zp2, zm2 = dev(x, y, wrap(z + 2, NZ), c), dev(x, y, wrap(z - 2, NZ), c)
+    give(2)
+    give(1)
+    keep(2)
+    give(3)
+    add(2)
+    ZP[3, lo] = CO[q4, lo].astype(BF16)
+    send(ZP.at[3, lo], P0, "ZP", 0, zp2)
+    ZM[3, hi] = CO[q4, hi].astype(BF16)
+    send(ZM.at[3, hi], M0, "ZM", 0, zm2)
+    keep(1)
+    add(1)
+    keep(3)
+    add(3)
+    for j in (0, 1, 2):
         qp, qm = wrap(z + 3 - j, NZ), wrap(z - 3 + j, NZ)
         for part, (sp, sm) in enumerate(((hi, lo), (lo, hi))):
-            recv(P.at[j - 1, sp], "ZP", 2 * j - 1 + part)
-            CO[qp, sp] = CO[qp, sp] + P[j - 1, sp]
-            send(CO.at[qp, sp], P.at[j, sp], "ZP", 2 * j + 1 + part, zp)
-            recv(M.at[j - 1, sm], "ZM", 2 * j - 1 + part)
-            CO[qm, sm] = CO[qm, sm] + M[j - 1, sm]
-            send(CO.at[qm, sm], M.at[j, sm], "ZM", 2 * j + 1 + part, zm)
+            vp = CO[qp, sp]
+            vm = CO[qm, sm]
+            if j > 0:
+                recv(P.at[j - 1, sp], "ZP", 2 * j - 1 + part)
+                vp = vp + P[j - 1, sp].astype(F32)
+            if j == 1 and part == 1:
+                recv(P0, "ZP", 0)
+                vp = vp + P0[...].astype(F32)
+            ZP[j, sp] = vp.astype(BF16)
+            send(ZP.at[j, sp], P.at[j, sp], "ZP", 2 * j + 1 + part, zp)
+            if j > 0:
+                recv(M.at[j - 1, sm], "ZM", 2 * j - 1 + part)
+                vm = vm + M[j - 1, sm].astype(F32)
+            if j == 1 and part == 1:
+                recv(M0, "ZM", 0)
+                vm = vm + M0[...].astype(F32)
+            ZM[j, sm] = vm.astype(BF16)
+            send(ZM.at[j, sm], M.at[j, sm], "ZM", 2 * j + 1 + part, zm)
+        if j == 0:
+            give(0)
+            keep(0)
+        if j == 1:
+            add(0)
+            for k in range(1, NZ):
+                q = wrap(z + k, NZ)
+                send(DS.at[q], DV.at[z], "DV", z, dev(x, y, q, c))
+            DV[z] = DS[z]
+    for k in range(1, NZ):
+        q = wrap(z + k, NZ)
+        recv(DV.at[q], "DV", q)
+    dv = DV[0]
+    for k in range(1, NZ):
+        dv = dv + DV[k]
+    diag = jnp.concatenate([dv] * 4, axis=1)
     for part, (sp, sm) in enumerate(((hi, lo), (lo, hi))):
         recv(P.at[2, sp], "ZP", 5 + part)
         recv(M.at[2, sm], "ZM", 5 + part)
-    cc = (CO[z] + (P[2] + M[2])) * (1.0 / N)
-
     ri = x * W + z * Q + lax.broadcasted_iota(jnp.int32, (Q, H), 0)
     ci = y * W + c * H + lax.broadcasted_iota(jnp.int32, (Q, H), 1)
+    cc = CO[z] + (P[2].astype(F32) + M[2].astype(F32))
+    cc = jnp.where(ri == ci, diag, cc) * (1.0 / N)
+
     g = jnp.where(ri == ci, -2.0 * (1.0 - cc), (2.0 * OFF_WEIGHT) * cc).astype(BF16)
     GT[c, rowsq(z)] = g
-    for part in (lo, hi):
-        src = GT.at[c, pl.ds(pl.multiple_of(z * Q + part.start, R), R)]
-        send(src, src, "G", 2 * z + part.start // R, zp)
-        send(src, src, "G", 2 * z + part.start // R, zm)
+    for first in (0, 1):
+        for h, to in ((first, zp), (1 - first, zm)):
+            src = GT.at[c, pl.ds(pl.multiple_of(z * Q + h * R, R), R)]
+            send(src, src, "G", 2 * z + h, to)
     src = GT.at[c, rowsq(z)]
     send(src, src, "GX", c * NZ + z, sib)
 
@@ -320,12 +357,14 @@
         return GT.at[c, pl.ds(pl.multiple_of(q * Q + h * R, R), R)]
 
     for j in (1, 2, 3):
-        for sgn, to in ((-1, zp), (1, zm)):
+        for sgn, to, to2, far in ((-1, zp, zp2, 0), (1, zm, zm2, 1)):
             q = wrap(z + sgn * j, NZ)
-            for h in (0, 1):
+            for h in (far, 1 - far):
                 recv(gpart(q, h), "G", 2 * q + h)
-                if j < 3 or (h == 0 if sgn < 0 else h == 1):
+                if j < 3:
                     send(gpart(q, h), gpart(q, h), "G", 2 * q + h, to)
+                if j == 2 and h == far:
+                    send(gpart(q, h), gpart(q, h), "G", 2 * q + h, to2)
             src = GT.at[c, rowsq(q)]
             send(src, src, "GX", c * NZ + q, sib)
     for h in (0, 1):
@@ -333,6 +372,33 @@
     src = GT.at[c, rowsq(q4)]
     send(src, src, "GX", c * NZ + q4, sib)
 
+    for q in range(NZ):
+        qq = wrap(z - q, NZ)
+        dst = GT.at[o, rowsq(qq)]
+        recv(dst, "GX", o * NZ + qq)
+
+    order = (2, 1, 3, 0)
+
+    def term_a(yy):
+        lhs = jnp.concatenate([TB[rows(slot(wrap(x + r, NX), yy)), :] for r in order], axis=0)
+        t = lax.dot_general(lhs[:, :H], GT[0], (((1,), (1,)), ((), ())), preferred_element_type=F32)
+        t = t + lax.dot_general(lhs[:, H:], GT[1], (((1,), (1,)), ((), ())), preferred_element_type=F32)
+        return SCALE * t
+
+    def term_b(xx):
+        lhs = jnp.concatenate([TA[rows(slot(xx, wrap(y + r, NY))), :] for r in order], axis=0)
+        return SCALE * jnp.concatenate(
+            [jnp.dot(lhs, GT[h], preferred_element_type=F32) for h in range(2)], axis=1)
+
+    sides = (
+        (term_a, y, NY, PA, AP0, AP, AM0, AM, "AP", "AM", yp, ym),
+        (term_b, x, NX, PB, BP0, BP, BM0, BM, "BP", "BM", xp, xm),
+    )
+    for term, pos, n, buf, p0, p1, m0, m1, fp, fm, to_p, to_m in sides:
+        buf[2] = term(wrap(pos + 2, n)).astype(BF16).reshape(4, R, W)
+        for i, (kp, km) in enumerate(((0, 1), (3, 2))):
+            send(buf.at[2, kp], p0.at[i], fp, i, to_p)
+            send(buf.at[2, km], m0.at[i], fm, i, to_m)
     for k, s in zc:
         i = wrap(z + k, NZ) * NC + (c + s) % NC
         recv(MO.at[i], "MO", i)
@@ -348,46 +414,22 @@
         send(MA.at[y], MA.at[y], "MA", y, dev(x, wrap(y + k, NY), z, c))
         send(MB.at[x], MB.at[x], "MB", x, dev(wrap(x + k, NX), y, z, c))
 
-    for q in range(NZ):
-        qq = wrap(z - q, NZ)
-        dst = GT.at[o, rowsq(qq)]
-        recv(dst, "GX", o * NZ + qq)
-
-    def term_a(yy):
-        lhs = jnp.concatenate([TB[rows(slot(k, yy)), :] for k in range(4)], axis=0)
-        t = lax.dot_general(lhs[:, :H], GT[0], (((1,), (1,)), ((), ())), preferred_element_type=F32)
-        t = t + lax.dot_general(lhs[:, H:], GT[1], (((1,), (1,)), ((), ())), preferred_element_type=F32)
-        return SCALE * t
-
-    def term_b(xx):
-        lhs = TA[pl.ds(pl.multiple_of(xx * 4 * R, 4 * R), 4 * R), :]
-        return SCALE * jnp.concatenate(
-            [jnp.dot(lhs, GT[h], preferred_element_type=F32) for h in range(2)], axis=1)
-
-    sides = (
-        (term_a, y, NY, PA, AP0, AP, AM0, AM, "AP", "AM", yp, ym),
-        (term_b, x, NX, PB, BP0, BP, BM0, BM, "BP", "BM", xp, xm),
-    )
-    for term, pos, n, buf, p0, p1, m0, m1, fp, fm, to_p, to_m in sides:
-        buf[2] = term(wrap(pos + 2, n)).astype(BF16).reshape(4, R, W)
-        for k in range(2):
-            send(buf.at[2, k], p0.at[k], fp, k, to_p)
-            send(buf.at[2, 2 + k], m0.at[k], fm, k, to_m)
     for term, pos, n, buf, p0, p1, m0, m1, fp, fm, to_p, to_m in sides:
         buf[0] = term(wrap(pos + 1, n)).astype(BF16).reshape(4, R, W)
-        for k in (2, 3):
-            send(buf.at[0, k], p1.at[k], fp, 2 + k, to_p)
-        for k in range(2):
-            recv(p0.at[k], fp, k)
-            buf[0, k] = (buf[0, k].astype(F32) + p0[k].astype(F32)).astype(BF16)
-            send(buf.at[0, k], p1.at[k], fp, 2 + k, to_p)
+        send(buf.at[0, 1], p1.at[1], fp, 3, to_p)
         buf[1] = term(wrap(pos - 1, n)).astype(BF16).reshape(4, R, W)
-        for k in range(2):
-            send(buf.at[1, k], m1.at[k], fm, 2 + k, to_m)
-        for k in range(2):
-            recv(m0.at[k], fm, k)
-            buf[1, 2 + k] = (buf[1, 2 + k].astype(F32) + m0[k].astype(F32)).astype(BF16)
-            send(buf.at[1, 2 + k], m1.at[2 + k], fm, 4 + k, to_m)
+        send(buf.at[1, 0], m1.at[0], fm, 2, to_m)
+    for i, (kp, km) in enumerate(((0, 1), (3, 2))):
+        for term, pos, n, buf, p0, p1, m0, m1, fp, fm, to_p, to_m in sides:
+            recv(p0.at[i], fp, i)
+            buf[0, kp] = (buf[0, kp].astype(F32) + p0[i].astype(F32)).astype(BF16)
+            send(buf.at[0, kp], p1.at[kp], fp, 2 + kp, to_p)
+            recv(m0.at[i], fm, i)
+            buf[1, km] = (buf[1, km].astype(F32) + m0[i].astype(F32)).astype(BF16)
+            send(buf.at[1, km], m1.at[km], fm, 2 + km, to_m)
+            if i == 0:
+                send(buf.at[0, 2], p1.at[2], fp, 4, to_p)
+                send(buf.at[1, 3], m1.at[3], fm, 5, to_m)
 
     for k in (1, 3, 2):
         recv(MA.at[wrap(y + k, NY)], "MA", wrap(y + k, NY))
@@ -399,22 +441,27 @@
     buf_b = term_b(x).astype(BF16)
     PA[3] = buf_a.reshape(4, R, W)
     PB[3] = buf_b.reshape(4, R, W)
-    for k in range(4):
+    for k, r in enumerate(order):
         recv(AP.at[k], "AP", 2 + k)
         recv(AM.at[k], "AM", 2 + k)
+        t = wrap(x + r, NX)
         back = PA[3, k].astype(F32) + (AP[k].astype(F32) + AM[k].astype(F32))
-        SA[k] = (FIN[1:2, :] * (back - TA[rows(slot(k, y)), :].astype(F32) * mom_a)).astype(BF16)
+        grad = (FIN[1:2, :] * (back - TA[rows(slot(t, y)), :].astype(F32) * mom_a)).astype(BF16)
+        if r:
+            SA[k] = grad
+            send(SA.at[k], ga.at[:, cols(x)], "OA", x, dev(t, y, z, c))
+        else:
+            ga[:, cols(x)] = grad
         recv(BP.at[k], "BP", 2 + k)
         recv(BM.at[k], "BM", 2 + k)
+        t = wrap(y + r, NY)
         back = PB[3, k].astype(F32) + (BP[k].astype(F32) + BM[k].astype(F32))
-        SB[k] = (FIN[3:4, :] * (back - TB[rows(slot(x, k)), :].astype(F32) * mom_b)).astype(BF16)
-    for k in (2, 1, 3):
-        t = wrap(x + k, NX)
-        send(SA.at[t], ga.at[:, cols(x)], "OA", x, dev(t, y, z, c))
-        t = wrap(y + k, NY)
-        send(SB.at[t], gb.at[:, cols(y)], "OB", y, dev(x, t, z, c))
-    ga[:, cols(x)] = SA[x]
-    gb[:, cols(y)] = SB[y]
+        grad = (FIN[3:4, :] * (back - TB[rows(slot(x, t)), :].astype(F32) * mom_b)).astype(BF16)
+        if r:
+            SB[k] = grad
+            send(SB.at[k], gb.at[:, cols(y)], "OB", y, dev(x, t, z, c))
+        else:
+            gb[:, cols(y)] = grad
     for k in (1, 3, 2):
         t = wrap(x + k, NX)
         recv(ga.at[:, cols(t)], "OA", t)
@@ -431,6 +478,7 @@
 def local(view_a, view_b):
     V = pltpu.VMEM
     scratch = [
+        V((R, D), BF16), V((R, D), BF16),
         V((16, R, W), BF16), V((16, R, W), BF16),
         V((16 * R, W), BF16), V((16 * R, W), BF16),
         V((4, 2, W), F32), V((4, 2, W), F32),
@@ -438,7 +486,9 @@
         V((4, 2, W), F32), V((4, 2, W), F32),
         V((16, 4, W), F32), V((4, W), F32),
         V((NZ, Q, H), F32), V((NZ, Q, H), F32), V((NZ, Q, H), F32),
-        V((R, H), F32), V((3, Q, H), F32), V((R, H), F32), V((3, Q, H), F32),
+        V((R, H), BF16), V((3, Q, H), BF16), V((R, H), BF16), V((3, Q, H), BF16),
+        V((4, Q, H), BF16), V((4, Q, H), BF16),
+        V((NZ, 1, Q), F32), V((NZ, 1, Q), F32),
         V((2, W, H), BF16),
         V((16, 8, 128), F32), V((4, 1, W), F32), V((4, 1, W), F32),
         V((4, 4, R, W), BF16), V((4, 4, R, W), BF16),
@@ -452,7 +502,7 @@
     return tuple(pl.pallas_call(
         kernel,
         out_shape=(out, out),
-        in_specs=[pl.BlockSpec(memory_space=pltpu.VMEM)] * 2,
+        in_specs=[pl.BlockSpec(memory_space=pl.ANY)] * 2,
         out_specs=(pl.BlockSpec(memory_space=pltpu.VMEM),) * 2,
         scratch_shapes=scratch,
         compiler_params=pltpu.CompilerParams(

time: 127 us -> 110 us (0.87)
  Pallas kernels: 123 us -> 106 us
    pallas_call x1, Pallas kernels: 123 us -> 106 us  [local(): pl.pallas_call(kernel, out_shape=(out, out), in_specs=[pl.BlockSpec(memor...]
where the time goes in v2:
time: 110 us; the launch traced here: 109 us
  Pallas kernels  106 us (96%)
  local copies, waits for them, and re-layouts  2.72 us (2%)
    pallas_call x1, Pallas kernels, local(): pl.pallas_call(kernel, out_shape=(out, out), in_specs=[pl.BlockSpec(memor...  106 us
    unnamed x4, local copies, waits for them, and re-layouts  2.72 us

profile of v2, /device:TPU:1, one launch (start us, length us, event | category | flops | bytes accessed | tf_op | source)
XLA Modules:
  0.0 109.3 jit_solution(163905954015317869)
XLA Ops:
  0.6 105.9 %shard_map.41 = (bf16[64,4096]{1,0:T(8,128)(2,1)}, bf16[64,4096]{1,0:T(8,128)(2,1)}) custom-call(bf16[64,4096]{1,0:T(8,128)(2,1)} %a_hbm.1, bf16[64,4096]{1,0:T(8,128)(2,1)} %b_hbm.1), custom_call_target="tpu_custom_call" | custom-call | tf_op jit(solution)/shard_map/pallas_call | solution.py:502
  106.6 0.0 copy-start
  106.6 1.9 %copy.6 = bf16[64,4096]{1,0:T(8,128)(2,1)} copy(bf16[64,4096]{1,0:T(8,128)(2,1)} %get-tuple-element.4) | data formatting | bytes 1048576
  108.5 0.0 copy-done
  108.5 0.8 copy.7
Async XLA Ops:
  106.6 1.9 %copy-start = (bf16[64,4096]{1,0:T(8,128)(2,1)S(1)}, bf16[64,4096]{1,0:T(8,128)(2,1)}, u32[]{:S(2)}) copy-start(bf16[64,4096]{1,0:T(8,128)(2,1)} %get-tuple-element.5) | copy-start | bytes 1572868

commit v3 on v0

v3 whole, which is shorter than its diff:
```python
import jax
import jax.numpy as jnp
from jax import lax
from jax.experimental import pallas as pl
from jax.experimental.pallas import tpu as pltpu
from jax.sharding import PartitionSpec as P

NX, NY, NZ, NC = 4, 4, 8, 2
R = 64
D = 4096
W = 1024
E = 256
T = 16
BLOCKS = ((0, 0), (1, 0), (0, 1), (1, 1), (2, 0), (0, 2), (2, 1), (1, 2), (2, 2),
          (3, 0), (0, 3), (3, 1), (1, 3), (3, 2), (2, 3), (3, 3))
POS = {ij: p for p, ij in enumerate(BLOCKS)}
SETS = ((0, 4), (4, 6), (6, 9), (9, 11), (11, 13), (13, 16))
RECTS = (((0, 2, 0, 2),), ((2, 1, 0, 1), (0, 1, 2, 1)), ((2, 1, 1, 2), (1, 1, 2, 1)),
         ((3, 1, 0, 1), (0, 1, 3, 1)), ((3, 1, 1, 1), (1, 1, 3, 1)), ((3, 1, 2, 2), (2, 1, 3, 1)))
STEPS = ((0, 512), (512, 256), (768, 256))
N = 16384
OFF_WEIGHT = 0.0051
EPS = 1e-05
SCALE = 16.0
F32 = jnp.float32
BF16 = jnp.bfloat16
MESH = pl.DeviceIdType.MESH

_SIZES = dict(
    A1=12, B1=12, A2=24, B2=24, S1A=4, S1B=4, S2A=4, S2B=4, SC=1, S3=8, CX=6,
    Z1P=12, Z1M=12, ZHP=6, ZHM=6, Z2P=6, Z2M=6, DV=32, GF=48, GH=12, GX=6, MS=1, MO=8, MA=4, MB=4,
    BH=32, BF=32, OA=16, OB=16, LOC=2,
)
SEM = {}
_n = 0
for _k, _v in _SIZES.items():
    SEM[_k] = _n
    _n += _v
N_RECV = _n
N_SEND = 340


def kernel(a_hbm, b_hbm, ga, gb, a_in, b_in, RA0, RA1, RA2, RB0, RB1, RB2, TA, TB, S0A, S0B, S1A, S1B, S2A, S2B, SC, S3, FIN,
           TT, C2, CR, CO, Z1P, Z1M, ZHP, ZHM, Z2P, Z2M, Y1P, Y1M, YHP, YHM, Y2P, Y2M, DS, DV, GS, ACC, MS, MO, MA, MB,
           PB, BH, BF,
           SA, SB, ssem, rsem):
    me = lax.axis_index("dp")
    c = lax.axis_index("mp")
    x = me // (NZ * NY)
    z = (me // NY) % NZ
    y = me % NY
    o = 1 - c

    def dev(xx, yy, zz, cc):
        return {"dp": xx * (NZ * NY) + zz * NY + yy, "mp": cc}

    def wrap(v, n):
        return (v + n) % n

    peers = [dev(wrap(x + k, NX), y, z, c) for k in range(1, NX)]
    peers += [dev(x, wrap(y + k, NY), z, c) for k in range(1, NY)]
    peers += [dev(x, y, wrap(z + k, NZ), c) for k in range(1, NZ)]
    peers += [dev(x, y, z, 1 - c)]
    barrier = pltpu.get_barrier_semaphore()
    for p in peers:
        pl.semaphore_signal(barrier, inc=1, device_id=p, device_id_type=MESH)
    la = pltpu.make_async_copy(a_hbm, a_in, rsem.at[SEM["LOC"]])
    lb = pltpu.make_async_copy(b_hbm, b_in, rsem.at[SEM["LOC"] + 1])
    la.start()
    lb.start()

    xp, xm = dev(wrap(x + 1, NX), y, z, c), dev(wrap(x - 1, NX), y, z, c)
    yp, ym = dev(x, wrap(y + 1, NY), z, c), dev(x, wrap(y - 1, NY), z, c)
    zp, zm = dev(x, y, wrap(z + 1, NZ), c), dev(x, y, wrap(z - 1, NZ), c)
    sib = dev(x, y, z, o)

    RA, RB = (RA0, RA1, RA2), (RB0, RB1, RB2)
    sent = []

    def send(src, dst, fam, idx, to):
        cp = pltpu.make_async_remote_copy(
            src_ref=src, dst_ref=dst, send_sem=ssem.at[len(sent)], recv_sem=rsem.at[SEM[fam] + idx],
            device_id=to, device_id_type=MESH)
        cp.start()
        sent.append(cp)

    def recv(dst, fam, idx):
        pltpu.make_async_remote_copy(
            src_ref=dst, dst_ref=dst, send_sem=ssem.at[0], recv_sem=rsem.at[SEM[fam] + idx],
            device_id=sib, device_id_type=MESH).wait_recv()

    def cols(i, w=W):
        return pl.ds(pl.multiple_of(i * w, w), w)

    def part_of(i, off, w):
        return pl.ds(pl.multiple_of(i * W + off, w), w)

    def slot(xx, yy):
        return yy * NX + xx

    def rows(s):
        return pl.ds(pl.multiple_of(s * R, R), R)

    def local_stats(v_ref, s_ref):
        for i in range(4):
            v = v_ref[:, i * W:(i + 1) * W].astype(F32)
            m = jnp.sum(v, axis=0, keepdims=True) * (1.0 / R)
            d = v - m
            s_ref[i, 0:1, :] = m
            s_ref[i, 1:2, :] = jnp.sum(d * d, axis=0, keepdims=True)

    la.wait()
    local_stats(a_in, S0A)
    for (off, w), buf in zip(STEPS, RA):
        buf[y * 4 + x] = a_in[:, part_of(x, off, w)]
    lb.wait()
    local_stats(b_in, S0B)
    for (off, w), buf in zip(STEPS, RB):
        buf[x * 4 + y] = b_in[:, part_of(y, off, w)]
    pl.semaphore_wait(barrier, len(peers))

    def f1(n):
        off, w = STEPS[n]
        for k in (2, 1, 3):
            t = wrap(x + k, NX)
            send(a_in.at[:, part_of(t, off, w)], RA[n].at[y * 4 + x], "A1", 4 * n + x, dev(t, y, z, c))
            t = wrap(y + k, NY)
            send(b_in.at[:, part_of(t, off, w)], RB[n].at[x * 4 + y], "B1", 4 * n + y, dev(x, t, z, c))

    def two(buf, w, h):
        return buf.at[pl.ds(pl.multiple_of(w * 4 + 2 * h, 2), 2)]

    def f2(n):
        for k in (1, 3, 2):
            t = wrap(x + k, NX)
            recv(RA[n].at[y * 4 + t], "A1", 4 * n + t)
            t = wrap(y + k, NY)
            recv(RB[n].at[x * 4 + t], "B1", 4 * n + t)
        for h in (0, 1):
            for buf, fam, w, to_p, to_m in ((RA[n], "A2", y, yp, ym), (RB[n], "B2", x, xp, xm)):
                a, b = two(buf, w, h), two(buf, w, 1 - h)
                send(a, a, fam, 8 * n + 2 * w + h, to_p)
                send(b, b, fam, 8 * n + 2 * w + 1 - h, to_m)

    views = (("A2", y, NY, yp, ym), ("B2", x, NX, xp, xm))

    def fw(n):
        for (fam, w, size, to_p, to_m), buf in zip(views, (RA[n], RB[n])):
            for h, t, to in ((0, wrap(w - 1, size), to_p), (1, wrap(w + 1, size), to_m)):
                a = two(buf, t, h)
                recv(a, fam, 8 * n + 2 * t + h)
                send(a, a, fam, 8 * n + 2 * t + h, to)

    def norm(n, ta, tb):
        off, w = STEPS[n]
        cs = slice(off, off + w)

        def body(i, _):
            v = (RA[n][ta * 4 + i].astype(F32) - FIN[0:1, cs]) * FIN[1:2, cs]
            TA[rows(slot(i, ta)), cs] = v.astype(BF16)
            v = (RB[n][tb * 4 + i].astype(F32) - FIN[2:3, cs]) * FIN[3:4, cs]
            TB[rows(slot(tb, i)), cs] = v.astype(BF16)
            return 0

        lax.fori_loop(0, 4, body, 0)
        at = pl.ds(pl.multiple_of(ta * 4 * R, 4 * R), 4 * R)
        TT[cs, at] = TA[at, cs].T

    def rest(n):
        norm(n, y, x)
        for (fam, w, size, _, _), buf in zip(views, (RA[n], RB[n])):
            for h, t in ((1, wrap(w - 1, size)), (0, wrap(w + 1, size))):
                recv(two(buf, t, h), fam, 8 * n + 2 * t + h)
        norm(n, wrap(y - 1, NY), wrap(x - 1, NX))
        norm(n, wrap(y + 1, NY), wrap(x + 1, NX))
        for (fam, w, size, _, _), buf in zip(views, (RA[n], RB[n])):
            t = wrap(w + 2, size)
            for h in (0, 1):
                recv(two(buf, t, h), fam, 8 * n + 2 * t + h)
        norm(n, wrap(y + 2, NY), wrap(x + 2, NX))

    def merge(parts, n):
        mean = parts[0][0]
        for m, _ in parts[1:]:
            mean = mean + m
        mean = mean * (1.0 / len(parts))
        total = None
        for m, q in parts:
            d = m - mean
            t = q + n * (d * d)
            total = t if total is None else total + t
        return mean, total

    def st1():
        for k in (2, 1, 3):
            t = wrap(x + k, NX)
            send(S0A.at[t], S1A.at[x], "S1A", x, dev(t, y, z, c))
            t = wrap(y + k, NY)
            send(S0B.at[t], S1B.at[y], "S1B", y, dev(x, t, z, c))
        S1A[x] = S0A[x]
        S1B[y] = S0B[y]

    def st2():
        for k in (1, 3, 2):
            recv(S1A.at[wrap(x + k, NX)], "S1A", wrap(x + k, NX))
            recv(S1B.at[wrap(y + k, NY)], "S1B", wrap(y + k, NY))
        for src, dst, w in ((S1A, S2A, y), (S1B, S2B, x)):
            mean, m2 = merge([(src[k, 0:1, :], src[k, 1:2, :]) for k in range(4)], float(R))
            dst[w, 0:1, :] = mean
            dst[w, 1:2, :] = m2
        for k in (2, 1, 3):
            send(S2A.at[y], S2A.at[y], "S2A", y, dev(x, wrap(y + k, NY), z, c))
            send(S2B.at[x], S2B.at[x], "S2B", x, dev(wrap(x + k, NX), y, z, c))

    def st3():
        for k in (1, 3, 2):
            recv(S2A.at[wrap(y + k, NY)], "S2A", wrap(y + k, NY))
            recv(S2B.at[wrap(x + k, NX)], "S2B", wrap(x + k, NX))
        for v, src in ((0, S2A), (1, S2B)):
            mean, m2 = merge([(src[k, 0:1, :], src[k, 1:2, :]) for k in range(4)], 4.0 * R)
            SC[c, 2 * v:2 * v + 1, :] = mean
            SC[c, 2 * v + 1:2 * v + 2, :] = m2
        send(SC.at[c], SC.at[c], "SC", 0, sib)

    def st4():
        recv(SC.at[o], "SC", 0)
        for v in (0, 1):
            mean, m2 = merge([(SC[k, 2 * v:2 * v + 1, :], SC[k, 2 * v + 1:2 * v + 2, :]) for k in range(2)], 16.0 * R)
            S3[z, 2 * v:2 * v + 1, :] = mean
            S3[z, 2 * v + 1:2 * v + 2, :] = m2
        for k in (4, 3, 5, 2, 6, 1, 7):
            send(S3.at[z], S3.at[z], "S3", z, dev(x, y, wrap(z + k, NZ), c))

    def st5():
        for k in (1, 7, 2, 6, 3, 5, 4):
            recv(S3.at[wrap(z + k, NZ)], "S3", wrap(z + k, NZ))
        for v in (0, 1):
            mean, m2 = merge([(S3[k, 2 * v:2 * v + 1, :], S3[k, 2 * v + 1:2 * v + 2, :]) for k in range(8)], 32.0 * R)
            FIN[2 * v:2 * v + 1, :] = mean
            FIN[2 * v + 1:2 * v + 2, :] = lax.rsqrt(m2 * (1.0 / N) + EPS)

    def comp(n):
        p0, p1 = SETS[n]
        for i, ni, j, nj in RECTS[n]:
            t = jnp.dot(TT[i * E:(i + ni) * E, :], TB[:, j * E:(j + nj) * E], preferred_element_type=F32)
            for a in range(ni):
                for b in range(nj):
                    C2[POS[i + a, j + b]] = t[a * E:(a + 1) * E, b * E:(b + 1) * E].reshape(2, NZ, T, E)
        send(C2.at[p0:p1, o], CR.at[p0:p1], "CX", n, sib)

    zz = lax.broadcasted_iota(jnp.int32, (T, E), 1) - lax.broadcasted_iota(jnp.int32, (T, E), 0)

    def add(n):
        p0, p1 = SETS[n]
        recv(CR.at[p0:p1], "CX", n)

        def body(p, _):
            CO[p] = C2[p, c] + CR[p]
            return 0

        lax.fori_loop(p0, p1, body, 0)
        for p in range(p0, p1):
            i, j = BLOCKS[p]
            if i == j:
                for q in range(NZ):
                    DS[i, q] = jnp.sum(jnp.where(zz == c * 128 + q * T, CO[p, q], 0.0), axis=0, keepdims=True)

    zp2, zm2 = dev(x, y, wrap(z + 2, NZ), c), dev(x, y, wrap(z - 2, NZ), c)
    q4 = (z + 4) % NZ

    def rs1(n):
        p0, p1 = SETS[n]
        sl = slice(p0, p1)
        v = CO[sl, q4].astype(BF16)
        ZHP[sl] = v[:, :, :128]
        ZHM[sl] = v[:, :, 128:]
        send(ZHP.at[sl], YHP.at[sl], "ZHP", n, zp2)
        send(ZHM.at[sl], YHM.at[sl], "ZHM", n, zm2)
        for k in (1, 0):
            d = 1 + 2 * k
            Z1P[k, sl] = CO[sl, wrap(z + d, NZ)].astype(BF16)
            send(Z1P.at[k, sl], Y1P.at[k, sl], "Z1P", 2 * n + k, zp)
            Z1M[k, sl] = CO[sl, wrap(z - d, NZ)].astype(BF16)
            send(Z1M.at[k, sl], Y1M.at[k, sl], "Z1M", 2 * n + k, zm)
        for p in range(p0, p1):
            i, j = BLOCKS[p]
            if i == j:
                for k in range(1, NZ):
                    q = wrap(z + k, NZ)
                    send(DS.at[i, q], DV.at[i, z], "DV", i * NZ + z, dev(x, y, q, c))
                DV[i, z] = DS[i, z]

    def rs2(n):
        sl = slice(*SETS[n])
        recv(YHP.at[sl], "ZHP", n)
        recv(Y1P.at[1, sl], "Z1P", 2 * n + 1)
        v = CO[sl, wrap(z + 2, NZ)] + Y1P[1, sl].astype(F32)
        h = YHP[sl].astype(F32)
        Z2P[sl] = jnp.concatenate([v[:, :, :128] + h, v[:, :, 128:]], axis=2).astype(BF16)
        send(Z2P.at[sl], Y2P.at[sl], "Z2P", n, zp2)
        recv(YHM.at[sl], "ZHM", n)
        recv(Y1M.at[1, sl], "Z1M", 2 * n + 1)
        v = CO[sl, wrap(z - 2, NZ)] + Y1M[1, sl].astype(F32)
        h = YHM[sl].astype(F32)
        Z2M[sl] = jnp.concatenate([v[:, :, :128], v[:, :, 128:] + h], axis=2).astype(BF16)
        send(Z2M.at[sl], Y2M.at[sl], "Z2M", n, zm2)

    def fin(n):
        p0, p1 = SETS[n]
        sl = slice(p0, p1)
        recv(Y1P.at[0, sl], "Z1P", 2 * n)
        recv(Y1M.at[0, sl], "Z1M", 2 * n)
        recv(Y2P.at[sl], "Z2P", n)
        recv(Y2M.at[sl], "Z2M", n)
        for p in range(p0, p1):
            i, j = BLOCKS[p]
            cc = CO[p, z] + ((Y1P[0, p].astype(F32) + Y1M[0, p].astype(F32)) + (Y2P[p].astype(F32) + Y2M[p].astype(F32)))
            if i == j:
                dv = DV[i, z]
                for k in range(1, NZ):
                    q = wrap(z + k, NZ)
                    recv(DV.at[i, q], "DV", i * NZ + q)
                    dv = dv + DV[i, q]
                on = jnp.logical_and(zz == c * 128 + z * T, x == y)
                cc = jnp.where(on, dv, cc) * (1.0 / N)
                g = jnp.where(on, -2.0 * (1.0 - cc), (2.0 * OFF_WEIGHT) * cc).astype(BF16)
            else:
                cc = cc * (1.0 / N)
                g = ((2.0 * OFF_WEIGHT) * cc).astype(BF16)
            GS[p, c, z] = g
            prod = g.astype(F32) * cc
            ACC[0, i] = ACC[0, i] + prod
            ACC[1, j] = ACC[1, j] + prod
        src = GS.at[sl, c, z]
        for k, to in ((0, zp), (2, zm)):
            send(src, src, "GF", 8 * n + k, to)

    def ag1(n):
        sl = slice(*SETS[n])
        for k, q, to in ((0, wrap(z - 1, NZ), zp), (2, wrap(z + 1, NZ), zm)):
            src = GS.at[sl, c, q]
            recv(src, "GF", 8 * n + k)
            send(src, src, "GF", 8 * n + k + 1, to)

    lanes_p, lanes_m = slice(0, 128), slice(128, 256)

    def ag2(n):
        sl = slice(*SETS[n])
        for k, q, to, to2, lanes in ((1, wrap(z - 2, NZ), zp, zp2, lanes_p), (3, wrap(z + 2, NZ), zm, zm2, lanes_m)):
            src = GS.at[sl, c, q]
            recv(src, "GF", 8 * n + k)
            half = GS.at[sl, c, q, :, lanes]
            send(half, half, "GH", 2 * n + k // 2, to2)
            send(src, src, "GF", 8 * n + 4 + k, to)

    def gx(n):
        sl = slice(*SETS[n])
        for k, q in ((5, wrap(z - 3, NZ)), (7, wrap(z + 3, NZ))):
            recv(GS.at[sl, c, q], "GF", 8 * n + k)
        recv(GS.at[sl, c, q4, :, lanes_p], "GH", 2 * n)
        recv(GS.at[sl, c, q4, :, lanes_m], "GH", 2 * n + 1)
        send(GS.at[sl, c], GS.at[sl, c], "GX", n, sib)

    def gx_wait(n):
        sl = slice(*SETS[n])
        recv(GS.at[sl, o], "GX", n)

    def mom1():
        for i in range(4):
            r = jnp.sum(ACC[0, i], axis=1, keepdims=True)
            MS[c, 0:1, i * E:(i + 1) * E] = jnp.sum(jnp.where(zz == c * 128 + z * T, r, 0.0), axis=0, keepdims=True)
            MS[c, 1:2, i * E:(i + 1) * E] = jnp.sum(ACC[1, i], axis=0, keepdims=True)
        send(MS.at[c], MS.at[c], "MS", 0, sib)

    def mom1b():
        recv(MS.at[o], "MS", 0)
        MO[z] = MS[0] + MS[1]
        for k in (4, 3, 5, 2, 6, 1, 7):
            send(MO.at[z], MO.at[z], "MO", z, dev(x, y, wrap(z + k, NZ), c))

    def mom2():
        for k in (1, 7, 2, 6, 3, 5, 4):
            recv(MO.at[wrap(z + k, NZ)], "MO", wrap(z + k, NZ))
        for r, dst in ((0, MA.at[y]), (1, MB.at[x])):
            t = MO[0, r:r + 1, :]
            for k in range(1, NZ):
                t = t + MO[k, r:r + 1, :]
            dst[...] = t
        for k in (2, 1, 3):
            send(MA.at[y], MA.at[y], "MA", y, dev(x, wrap(y + k, NY), z, c))
            send(MB.at[x], MB.at[x], "MB", x, dev(wrap(x + k, NX), y, z, c))

    def mom3():
        for k in (1, 3, 2):
            recv(MA.at[wrap(y + k, NY)], "MA", wrap(y + k, NY))
            recv(MB.at[wrap(x + k, NX)], "MB", wrap(x + k, NX))
        FIN[4:5, :] = ((MA[0] + MA[1]) + (MA[2] + MA[3])) * SCALE
        FIN[5:6, :] = ((MB[0] + MB[1]) + (MB[2] + MB[3])) * SCALE

    def part(v, u, first, w):
        h = slice(0, 2) if first else slice(2, 4)
        return PB.at[v, u, w, h] if v == 0 else PB.at[v, u, h, w]

    def ways(v):
        return (y, NY, yp, ym) if v == 0 else (x, NX, xp, xm)

    def bw1(v, u):
        t = None
        for k in range(4):
            if v == 0:
                g = GS[POS[u, k]].reshape(E, E)
                d = lax.dot_general(TB[:, k * E:(k + 1) * E], g, (((1,), (1,)), ((), ())), preferred_element_type=F32)
            else:
                g = GS[POS[k, u]].reshape(E, E)
                d = jnp.dot(TA[:, k * E:(k + 1) * E], g, preferred_element_type=F32)
            t = d if t is None else t + d
        PB[v, u] = (SCALE * t).astype(BF16).reshape(4, 4, R, E)
        pos, n, to_p, to_m = ways(v)
        i = 8 * v + 2 * u
        send(part(v, u, True, wrap(pos + 2, n)), BH.at[v, u, 0], "BH", i, to_p)
        send(part(v, u, False, wrap(pos + 2, n)), BH.at[v, u, 1], "BH", i + 1, to_m)
        send(part(v, u, False, wrap(pos + 1, n)), BF.at[v, u, 0, 2:4], "BF", 2 * i + 1, to_p)
        send(part(v, u, True, wrap(pos - 1, n)), BF.at[v, u, 1, 0:2], "BF", 2 * i + 2, to_m)

    def bw2(v, u):
        pos, n, to_p, to_m = ways(v)
        i = 8 * v + 2 * u
        recv(BH.at[v, u, 0], "BH", i)
        src = part(v, u, True, wrap(pos + 1, n))
        src[...] = (src[...].astype(F32) + BH[v, u, 0].astype(F32)).astype(BF16)
        send(src, BF.at[v, u, 0, 0:2], "BF", 2 * i, to_p)
        recv(BH.at[v, u, 1], "BH", i + 1)
        src = part(v, u, False, wrap(pos - 1, n))
        src[...] = (src[...].astype(F32) + BH[v, u, 1].astype(F32)).astype(BF16)
        send(src, BF.at[v, u, 1, 2:4], "BF", 2 * i + 3, to_m)

    def out(v, u):
        i = 2 * (8 * v + 2 * u)
        for k in range(4):
            recv(BF.at[v, u, k // 2, (k % 2) * 2:(k % 2) * 2 + 2], "BF", i + k)
        w = slice(u * E, (u + 1) * E)
        for r in (2, 1, 3, 0):
            if v == 0:
                t = wrap(x + r, NX)
                mine_ = PB[0, u, y, t]
                norm = TA[rows(slot(t, y)), w]
                m, rs = FIN[4:5, w], FIN[1:2, w]
                dst = ga.at[:, pl.ds(pl.multiple_of(x * W + u * E, E), E)]
                fam, at, to = "OA", 4 * u + x, dev(t, y, z, c)
            else:
                t = wrap(y + r, NY)
                mine_ = PB[1, u, t, x]
                norm = TB[rows(slot(x, t)), w]
                m, rs = FIN[5:6, w], FIN[3:4, w]
                dst = gb.at[:, pl.ds(pl.multiple_of(y * W + u * E, E), E)]
                fam, at, to = "OB", 4 * u + y, dev(x, t, z, c)
            back = mine_.astype(F32) + (BF[v, u, 0, t].astype(F32) + BF[v, u, 1, t].astype(F32))
            grad = (rs * (back - norm.astype(F32) * m)).astype(BF16)
            if r:
                buf = SA if v == 0 else SB
                buf[u, r] = grad
                send(buf.at[u, r], dst, fam, at, to)
            else:
                dst[...] = grad

    ACC[...] = jnp.zeros_like(ACC)
    f1(0)
    st1()
    f1(1)
    f1(2)
    st2()
    f2(0)
    f2(1)
    st3()
    fw(0)
    st4()
    fw(1)
    f2(2)
    st5()
    rest(0)
    comp(0)
    rest(1)
    comp(1)
    comp(2)
    fw(2)
    add(0)
    rs1(0)
    add(1)
    add(2)
    rs1(1)
    rs1(2)
    rest(2)
    comp(3)
    rs2(0)
    comp(4)
    rs2(1)
    add(3)
    rs1(3)
    add(4)
    rs1(4)
    rs2(2)
    fin(0)
    comp(5)
    rs2(3)
    fin(1)
    rs2(4)
    add(5)
    rs1(5)
    fin(2)
    ag1(1)
    fin(3)
    ag1(0)
    fin(4)
    rs2(5)
    ag1(2)
    ag1(3)
    ag2(1)
    ag1(4)
    ag2(0)
    ag2(3)
    fin(5)
    gx(1)
    ag2(4)
    ag2(2)
    gx_wait(1)
    gx(0)
    gx(3)
    ag1(5)
    gx_wait(0)
    gx_wait(3)
    bw1(0, 0)
    bw1(1, 0)
    gx(4)
    gx(2)
    ag2(5)
    mom1()
    mom1b()
    gx_wait(2)
    gx_wait(4)
    bw1(0, 1)
    bw1(1, 1)
    bw2(0, 0)
    bw2(1, 0)
    gx(5)
    gx_wait(5)
    bw1(0, 3)
    bw1(1, 3)
    bw1(1, 2)
    bw1(0, 2)
    mom2()
    bw2(1, 1)
    bw2(0, 1)
    bw2(0, 3)
    bw2(1, 3)
    bw2(0, 2)
    bw2(1, 2)
    mom3()
    out(0, 0)
    out(1, 0)
    out(0, 1)
    out(1, 1)
    out(1, 3)
    out(0, 3)
    out(1, 2)
    out(0, 2)
    for u in range(4):
        for k in (1, 3, 2):
            t = wrap(x + k, NX)
            recv(ga.at[:, pl.ds(pl.multiple_of(t * W + u * E, E), E)], "OA", 4 * u + t)
            t = wrap(y + k, NY)
            recv(gb.at[:, pl.ds(pl.multiple_of(t * W + u * E, E), E)], "OB", 4 * u + t)
    for cp in sent:
        cp.wait_send()


def local(view_a, view_b):
    V = pltpu.VMEM
    scratch = [
        V((R, D), BF16), V((R, D), BF16),
        *[V((16, R, w), BF16) for _ in range(2) for _, w in STEPS],
        V((16 * R, W), BF16), V((16 * R, W), BF16),
        V((4, 2, W), F32), V((4, 2, W), F32),
        V((4, 2, W), F32), V((4, 2, W), F32),
        V((4, 2, W), F32), V((4, 2, W), F32),
        V((2, 4, W), F32), V((8, 4, W), F32), V((6, W), F32),
        V((W, W), BF16),
        V((16, 2, NZ, T, E), F32), V((16, NZ, T, E), F32), V((16, NZ, T, E), F32),
        V((2, 16, T, E), BF16), V((2, 16, T, E), BF16),
        V((16, T, 128), BF16), V((16, T, 128), BF16),
        V((16, T, E), BF16), V((16, T, E), BF16),
        V((2, 16, T, E), BF16), V((2, 16, T, E), BF16),
        V((16, T, 128), BF16), V((16, T, 128), BF16),
        V((16, T, E), BF16), V((16, T, E), BF16),
        V((4, NZ, 1, E), F32), V((4, NZ, 1, E), F32),
        V((16, 2, NZ, T, E), BF16), V((2, 4, T, E), F32),
        V((2, 2, W), F32), V((8, 2, W), F32), V((4, 1, W), F32), V((4, 1, W), F32),
        V((2, 4, 4, 4, R, E), BF16),
        V((2, 4, 2, 2, R, E), BF16), V((2, 4, 2, 4, R, E), BF16),
        V((4, 4, R, E), BF16), V((4, 4, R, E), BF16),
        pltpu.SemaphoreType.DMA((N_SEND,)),
        pltpu.SemaphoreType.DMA((N_RECV,)),
    ]
    out = pltpu.VMEM((R, D), BF16)
    return tuple(pl.pallas_call(
        kernel,
        out_shape=(out, out),
        in_specs=[pl.BlockSpec(memory_space=pl.ANY)] * 2,
        out_specs=(pl.BlockSpec(memory_space=pltpu.VMEM),) * 2,
        scratch_shapes=scratch,
        compiler_params=pltpu.CompilerParams(
            collective_id=0, has_side_effects=True, vmem_limit_bytes=56 * 1024 * 1024),
    )(view_a, view_b))


def solution(mesh):
    spec = P(("dp", "mp"), None)
    return jax.shard_map(local, mesh=mesh, in_specs=(spec, spec), out_specs=(spec, spec), check_vma=False)
```

time: 905 us -> 99.3 us (0.11)
  blocking collectives: 425 us -> 0 us
  waiting for transfers between devices: 385 us -> 0 us
  Pallas kernels: 0 us -> 96.9 us
  starting transfers between devices: 34.3 us -> 0 us
  matrix products: 21.1 us -> 0 us
  other arithmetic: 16.4 us -> 0 us
  between operations: 14.2 us -> 0.64 us
    all_to_all x3 -> x0, waiting for transfers between devices: 356 us -> none  [the longest x1 178 us: local(): lax.all_to_all(back_a.reshape(data_count, pair_rows, width_a), 'dp', spli...]
    psum x3 -> x0, blocking collectives: 232 us -> none  [the longest x1 81.6 us: local(): lax.psum((jnp.sum(values_a, axis=0), jnp.sum(values_b, axis=0)), ('dp', '...]
    all_to_all x1 -> x0, blocking collectives: 193 us -> none  [local(): lax.all_to_all(outgoing_a, 'dp', split_axis=0, concat_axis=0, tiled=True)]
    pallas_call x0 -> x1, Pallas kernels: none -> 96.9 us  [local(): pl.pallas_call(kernel, out_shape=(out, out), in_specs=[pl.BlockSpec(memor...]
    all_to_all x3 -> x0, starting transfers between devices: 34.3 us -> none  [the longest x1 14.1 us: local(): lax.all_to_all(back_b.reshape(data_count, pair_rows, width_b), 'dp', spli...]
    psum x1 -> x0, waiting for transfers between devices: 29.4 us -> none  [local(): correlation = lax.psum(partial_corr, 'mp') / total_rows]
    dot_general x3 -> x0, matrix products: 21.1 us -> none  [the longest x1 7.91 us: local(): jnp.einsum('nr,rc->nc', tile_norm_a, grad_corr, preferred_element_type=jn...]
    reduce_sum x8 -> x0, other arithmetic: 13 us -> none  [the longest x1 4.84 us: local(): jnp.sum(returned_a.astype(jnp.float32).reshape(GROUPS_A, column_groups, p...]
  transfers between devices with their start and end apart: 4 -> 0, of which waited for: 4 -> 0; matrix products, arithmetic and copies ran while one was open for 1% -> 0% of each run, Pallas kernels for 0% -> 0%
where the time goes in v3:
time: 99.3 us; the launch traced here: 99.2 us
  Pallas kernels  96.9 us (98%)
  local copies, waits for them, and re-layouts  1.59 us (2%)
    pallas_call x1, Pallas kernels, local(): pl.pallas_call(kernel, out_shape=(out, out), in_specs=[pl.BlockSpec(memor...  96.9 us

profile of v3, /device:TPU:1, one launch (start us, length us, event | category | flops | bytes accessed | tf_op | source)
XLA Modules:
  0.0 99.2 jit_solution(18333174435072104897)
XLA Ops:
  0.6 96.9 %shard_map.41 = (bf16[64,4096]{1,0:T(8,128)(2,1)S(1)}, bf16[64,4096]{1,0:T(8,128)(2,1)S(1)}) custom-call(bf16[64,4096]{1,0:T(8,128)(2,1)} %a_hbm.1, bf16[64,4096]{1,0:T(8,128)(2,1)} %b_hbm.1), custom_call_target="tpu_custom_call" | custom-call | tf_op jit(solution)/shard_map/pallas_call | solution.py:604
  97.6 0.8 copy.6
  98.4 0.8 copy.7

commit v4 on v3

--- a/solution.py
+++ b/solution.py
@@ -11,12 +11,13 @@
 W = 1024
 E = 256
 T = 16
-BLOCKS = ((0, 0), (1, 0), (0, 1), (1, 1), (2, 0), (0, 2), (2, 1), (1, 2), (2, 2),
-          (3, 0), (0, 3), (3, 1), (1, 3), (3, 2), (2, 3), (3, 3))
+BLOCKS = ((0, 0), (1, 0), (0, 1), (1, 1), (2, 0), (0, 2), (3, 0), (0, 3), (2, 1),
+          (1, 2), (3, 1), (1, 3), (2, 2), (3, 2), (2, 3), (3, 3))
 POS = {ij: p for p, ij in enumerate(BLOCKS)}
-SETS = ((0, 4), (4, 6), (6, 9), (9, 11), (11, 13), (13, 16))
-RECTS = (((0, 2, 0, 2),), ((2, 1, 0, 1), (0, 1, 2, 1)), ((2, 1, 1, 2), (1, 1, 2, 1)),
-         ((3, 1, 0, 1), (0, 1, 3, 1)), ((3, 1, 1, 1), (1, 1, 3, 1)), ((3, 1, 2, 2), (2, 1, 3, 1)))
+SETS = ((0, 4), (4, 6), (6, 8), (8, 10), (10, 12), (12, 13), (13, 16))
+RECTS = (((0, 2, 0, 2),), ((2, 1, 0, 1), (0, 1, 2, 1)), ((3, 1, 0, 1), (0, 1, 3, 1)), ((2, 1, 1, 1), (1, 1, 2, 1)),
+        ((3, 1, 1, 1), (1, 1, 3, 1)), ((2, 1, 2, 1),), ((3, 1, 2, 2), (2, 1, 3, 1)))
+SHORT = (2, 3, 5, 6)
 STEPS = ((0, 512), (512, 256), (768, 256))
 N = 16384
 OFF_WEIGHT = 0.0051
@@ -27,8 +28,8 @@
 MESH = pl.DeviceIdType.MESH
 
 _SIZES = dict(
-    A1=12, B1=12, A2=24, B2=24, S1A=4, S1B=4, S2A=4, S2B=4, SC=1, S3=8, CX=6,
-    Z1P=12, Z1M=12, ZHP=6, ZHM=6, Z2P=6, Z2M=6, DV=32, GF=48, GH=12, GX=6, MS=1, MO=8, MA=4, MB=4,
+    A1=12, B1=12, A2=24, B2=24, S1A=4, S1B=4, S2A=4, S2B=4, SC=1, S3=8, CX=7,
+    Z1P=14, Z1M=14, ZHP=7, ZHM=7, Z2P=7, Z2M=7, DV=32, GF=56, GH=14, GX=7, MS=1, MO=8, MA=4, MB=4,
     BH=32, BF=32, OA=16, OB=16, LOC=2,
 )
 SEM = {}
@@ -37,7 +38,7 @@
     SEM[_k] = _n
     _n += _v
 N_RECV = _n
-N_SEND = 340
+N_SEND = 360
 
 
 def kernel(a_hbm, b_hbm, ga, gb, a_in, b_in, RA0, RA1, RA2, RB0, RB1, RB2, TA, TB, S0A, S0B, S1A, S1B, S2A, S2B, SC, S3, FIN,
@@ -332,7 +333,8 @@
             ACC[0, i] = ACC[0, i] + prod
             ACC[1, j] = ACC[1, j] + prod
         src = GS.at[sl, c, z]
-        for k, to in ((0, zp), (2, zm)):
+        ways_ = ((1, zp2), (3, zm2), (0, zp), (2, zm)) if n in SHORT else ((0, zp), (2, zm))
+        for k, to in ways_:
             send(src, src, "GF", 8 * n + k, to)
 
     def ag1(n):
@@ -355,7 +357,8 @@
 
     def gx(n):
         sl = slice(*SETS[n])
-        for k, q in ((5, wrap(z - 3, NZ)), (7, wrap(z + 3, NZ))):
+        near = ((0, wrap(z - 1, NZ)), (2, wrap(z + 1, NZ))) if n in SHORT else ()
+        for k, q in near + ((5, wrap(z - 3, NZ)), (7, wrap(z + 3, NZ))):
             recv(GS.at[sl, c, q], "GF", 8 * n + k)
         recv(GS.at[sl, c, q4, :, lanes_p], "GH", 2 * n)
         recv(GS.at[sl, c, q4, :, lanes_m], "GH", 2 * n + 1)
@@ -464,105 +467,110 @@
                 dst[...] = grad
 
     ACC[...] = jnp.zeros_like(ACC)
+    st1()
     f1(0)
-    st1()
     f1(1)
+    st2()
     f1(2)
-    st2()
     f2(0)
+    st3()
+    st4()
+    fw(0)
     f2(1)
-    st3()
-    fw(0)
-    st4()
-    fw(1)
     f2(2)
     st5()
     rest(0)
     comp(0)
+    fw(1)
+    add(0)
+    rs1(0)
+    fw(2)
     rest(1)
     comp(1)
+    rs2(0)
+    rest(2)
     comp(2)
-    fw(2)
-    add(0)
-    rs1(0)
     add(1)
+    rs1(1)
+    comp(3)
+    comp(4)
     add(2)
-    rs1(1)
     rs1(2)
-    rest(2)
-    comp(3)
-    rs2(0)
-    comp(4)
-    rs2(1)
+    comp(5)
     add(3)
     rs1(3)
     add(4)
     rs1(4)
+    rs2(1)
+    add(5)
+    comp(6)
+    rs1(5)
     rs2(2)
     fin(0)
-    comp(5)
+    add(6)
+    rs1(6)
+    rs2(4)
     rs2(3)
     fin(1)
-    rs2(4)
-    add(5)
-    rs1(5)
+    ag1(0)
     fin(2)
+    rs2(6)
+    rs2(5)
     ag1(1)
+    fin(4)
+    ag2(0)
     fin(3)
-    ag1(0)
-    fin(4)
-    rs2(5)
-    ag1(2)
-    ag1(3)
     ag2(1)
+    ag2(2)
     ag1(4)
-    ag2(0)
+    fin(5)
+    gx(0)
+    fin(6)
     ag2(3)
-    fin(5)
     gx(1)
+    gx_wait(0)
+    gx(2)
     ag2(4)
-    ag2(2)
+    mom1()
     gx_wait(1)
-    gx(0)
+    gx_wait(2)
+    bw1(1, 0)
+    ag2(6)
+    bw1(0, 0)
+    ag2(5)
     gx(3)
-    ag1(5)
-    gx_wait(0)
+    gx(4)
     gx_wait(3)
-    bw1(0, 0)
-    bw1(1, 0)
-    gx(4)
-    gx(2)
-    ag2(5)
-    mom1()
     mom1b()
-    gx_wait(2)
     gx_wait(4)
     bw1(0, 1)
+    bw2(1, 0)
+    gx(6)
     bw1(1, 1)
-    bw2(0, 0)
-    bw2(1, 0)
     gx(5)
-    gx_wait(5)
+    gx_wait(6)
     bw1(0, 3)
     bw1(1, 3)
+    gx_wait(5)
+    bw1(0, 2)
     bw1(1, 2)
-    bw1(0, 2)
+    bw2(0, 0)
     mom2()
+    bw2(0, 3)
+    bw2(0, 2)
+    bw2(1, 3)
+    bw2(0, 1)
     bw2(1, 1)
-    bw2(0, 1)
-    bw2(0, 3)
-    bw2(1, 3)
-    bw2(0, 2)
     bw2(1, 2)
     mom3()
+    out(1, 0)
     out(0, 0)
-    out(1, 0)
+    out(0, 3)
+    out(1, 3)
+    out(0, 2)
+    out(1, 1)
+    out(1, 2)
     out(0, 1)
-    out(1, 1)
-    out(1, 3)
-    out(0, 3)
-    out(1, 2)
-    out(0, 2)
     for u in range(4):
         for k in (1, 3, 2):
             t = wrap(x + k, NX)

time: 99.3 us -> 96.2 us (0.969)
  Pallas kernels: 96.9 us -> 93.9 us
    pallas_call x1, Pallas kernels: 96.9 us -> 93.9 us  [local(): pl.pallas_call(kernel, out_shape=(out, out), in_specs=[pl.BlockSpec(memor...]
where the time goes in v4:
time: 96.2 us; the launch traced here: 96.1 us
  Pallas kernels  93.9 us (98%)
  local copies, waits for them, and re-layouts  1.59 us (2%)
    pallas_call x1, Pallas kernels, local(): pl.pallas_call(kernel, out_shape=(out, out), in_specs=[pl.BlockSpec(memor...  93.9 us

profile of v4, /device:TPU:1, one launch (start us, length us, event | category | flops | bytes accessed | tf_op | source)
XLA Modules:
  0.0 96.1 jit_solution(11128523637499812124)
XLA Ops:
  0.6 93.9 %shard_map.41 = (bf16[64,4096]{1,0:T(8,128)(2,1)S(1)}, bf16[64,4096]{1,0:T(8,128)(2,1)S(1)}) custom-call(bf16[64,4096]{1,0:T(8,128)(2,1)} %a_hbm.1, bf16[64,4096]{1,0:T(8,128)(2,1)} %b_hbm.1), custom_call_target="tpu_custom_call" | custom-call | tf_op jit(solution)/shard_map/pallas_call | solution.py:612
  94.5 0.8 copy.6
  95.3 0.8 copy.7

commit v5 on v4

--- a/solution.py
+++ b/solution.py
@@ -470,8 +470,8 @@
     st1()
     f1(0)
     f1(1)
+    f1(2)
     st2()
-    f1(2)
     f2(0)
     st3()
     st4()
@@ -558,9 +558,9 @@
     mom2()
     bw2(0, 3)
     bw2(0, 2)
-    bw2(1, 3)
     bw2(0, 1)
     bw2(1, 1)
+    bw2(1, 3)
     bw2(1, 2)
     mom3()
     out(1, 0)

time: 96.2 us -> 95.7 us (level)
  no operation moved by 1% of the time
where the time goes in v5:
time: 95.7 us; the launch traced here: 95.6 us
  Pallas kernels  93.4 us (98%)
  local copies, waits for them, and re-layouts  1.59 us (2%)
    pallas_call x1, Pallas kernels, local(): pl.pallas_call(kernel, out_shape=(out, out), in_specs=[pl.BlockSpec(memor...  93.4 us

profile of v5, /device:TPU:1, one launch (start us, length us, event | category | flops | bytes accessed | tf_op | source)
XLA Modules:
  0.0 95.6 jit_solution(16102076849795706876)
XLA Ops:
  0.6 93.4 %shard_map.41 = (bf16[64,4096]{1,0:T(8,128)(2,1)S(1)}, bf16[64,4096]{1,0:T(8,128)(2,1)S(1)}) custom-call(bf16[64,4096]{1,0:T(8,128)(2,1)} %a_hbm.1, bf16[64,4096]{1,0:T(8,128)(2,1)} %b_hbm.1), custom_call_target="tpu_custom_call" | custom-call | tf_op jit(solution)/shard_map/pallas_call | solution.py:612
  94.0 0.8 copy.6
  94.8 0.8 copy.7

commit v6 on v5

--- a/solution.py
+++ b/solution.py
@@ -269,6 +269,10 @@
     zp2, zm2 = dev(x, y, wrap(z + 2, NZ), c), dev(x, y, wrap(z - 2, NZ), c)
     q4 = (z + 4) % NZ
 
+    def diagonals(n):
+        on = sorted(i for i, j in BLOCKS[SETS[n][0]:SETS[n][1]] if i == j)
+        return slice(on[0], on[-1] + 1) if on else None
+
     def rs1(n):
         p0, p1 = SETS[n]
         sl = slice(p0, p1)
@@ -283,12 +287,12 @@
             send(Z1P.at[k, sl], Y1P.at[k, sl], "Z1P", 2 * n + k, zp)
             Z1M[k, sl] = CO[sl, wrap(z - d, NZ)].astype(BF16)
             send(Z1M.at[k, sl], Y1M.at[k, sl], "Z1M", 2 * n + k, zm)
-        for p in range(p0, p1):
-            i, j = BLOCKS[p]
-            if i == j:
-                for k in range(1, NZ):
-                    q = wrap(z + k, NZ)
-                    send(DS.at[i, q], DV.at[i, z], "DV", i * NZ + z, dev(x, y, q, c))
+        ds = diagonals(n)
+        if ds is not None:
+            for k in range(1, NZ):
+                q = wrap(z + k, NZ)
+                send(DS.at[ds, q], DV.at[ds, z], "DV", ds.start * NZ + z, dev(x, y, q, c))
+            for i in range(ds.start, ds.stop):
                 DV[i, z] = DS[i, z]
 
     def rs2(n):
@@ -313,6 +317,11 @@
         recv(Y1M.at[0, sl], "Z1M", 2 * n)
         recv(Y2P.at[sl], "Z2P", n)
         recv(Y2M.at[sl], "Z2M", n)
+        ds = diagonals(n)
+        if ds is not None:
+            for k in range(1, NZ):
+                q = wrap(z + k, NZ)
+                recv(DV.at[ds, q], "DV", ds.start * NZ + q)
         for p in range(p0, p1):
             i, j = BLOCKS[p]
             cc = CO[p, z] + ((Y1P[0, p].astype(F32) + Y1M[0, p].astype(F32)) + (Y2P[p].astype(F32) + Y2M[p].astype(F32)))
@@ -320,7 +329,6 @@
                 dv = DV[i, z]
                 for k in range(1, NZ):
                     q = wrap(z + k, NZ)
-                    recv(DV.at[i, q], "DV", i * NZ + q)
                     dv = dv + DV[i, q]
                 on = jnp.logical_and(zz == c * 128 + z * T, x == y)
                 cc = jnp.where(on, dv, cc) * (1.0 / N)

time: 95.7 us -> 95.7 us (level)
  no operation moved by 1% of the time
where the time goes in v6:
time: 95.7 us; the launch traced here: 95.6 us
  Pallas kernels  93.4 us (98%)
  local copies, waits for them, and re-layouts  1.59 us (2%)
    pallas_call x1, Pallas kernels, local(): pl.pallas_call(kernel, out_shape=(out, out), in_specs=[pl.BlockSpec(memor...  93.4 us

profile of v6, /device:TPU:1, one launch (start us, length us, event | category | flops | bytes accessed | tf_op | source)
XLA Modules:
  0.0 95.6 jit_solution(3664900499163651922)
XLA Ops:
  0.6 93.4 %shard_map.41 = (bf16[64,4096]{1,0:T(8,128)(2,1)S(1)}, bf16[64,4096]{1,0:T(8,128)(2,1)S(1)}) custom-call(bf16[64,4096]{1,0:T(8,128)(2,1)} %a_hbm.1, bf16[64,4096]{1,0:T(8,128)(2,1)} %b_hbm.1), custom_call_target="tpu_custom_call" | custom-call | tf_op jit(solution)/shard_map/pallas_call | solution.py:620
  94.0 0.8 copy.6
  94.8 0.8 copy.7
